TPU v7x, 32 devices: a whole 2x2x4 slice. The times are simulated.
32 devices in a mesh: seq: 4 (over y, x), batch: 8 (over z, core).
Axes of the slice: x: 2, y: 2, z: 4, core: 2. Of those that a mesh axis runs over, the one named last changes fastest.
Arguments:
- tokens: bfloat16 [2, 32, 1024, 1280], P(None, 'batch', 'seq'), may hold values from -8 to 8
- lengths: int32 [2, 32], P(None, 'batch'), may hold values from 30 to 1024, as said below
- first_gain: bfloat16 [1280], P('batch'), may hold values from 0.5 to 1.5
- first_shift: bfloat16 [1280], P('batch'), may hold values from -1.25 to 1.25
- down_weight: bfloat16 [1280, 640], P('seq', 'batch'), may hold values from -0.15625 to 0.15625
- down_bias: bfloat16 [640], P('batch'), may hold values from -1.25 to 1.25
- middle_gain: bfloat16 [640], P('batch'), may hold values from 0.5 to 1.5
- middle_shift: bfloat16 [640], P('batch'), may hold values from -1.25 to 1.25
- conv_weight: bfloat16 [5, 640, 640], P(None, 'seq', 'batch'), may hold values from -0.109375 to 0.109375
- conv_bias: bfloat16 [640], P('batch'), may hold values from -1.25 to 1.25
- final_gain: bfloat16 [640], P('batch'), may hold values from 0.5 to 1.5
- final_shift: bfloat16 [640], P('batch'), may hold values from -1.25 to 1.25
- up_weight: bfloat16 [640, 1280], P('seq', 'batch'), may hold values from -0.25 to 0.25
- up_bias: bfloat16 [1280], P('batch'), may hold values from -1.25 to 1.25
- cotangent: bfloat16 [2, 32, 1024, 1280], P(None, 'batch', 'seq'), may hold values from -8 to 8
Outputs:
- block_output: bfloat16 [2, 32, 1024, 1280], P(None, 'batch', 'seq')
- tokens_grad: bfloat16 [2, 32, 1024, 1280], P(None, 'batch', 'seq')
- first_gain_grad: float32 [1280], P('batch')
- first_shift_grad: float32 [1280], P('batch')
- down_weight_grad: float32 [1280, 640], P('seq', 'batch')
- down_bias_grad: float32 [640], P('batch')
- middle_gain_grad: float32 [640], P('batch')
- middle_shift_grad: float32 [640], P('batch')
- conv_weight_grad: float32 [5, 640, 640], P(None, 'seq', 'batch')
- conv_bias_grad: float32 [640], P('batch')
- final_gain_grad: float32 [640], P('batch')
- final_shift_grad: float32 [640], P('batch')
- up_weight_grad: float32 [640, 1280], P('seq', 'batch')
- up_bias_grad: float32 [1280], P('batch')
Inputs may be any that keep to these rules, and one draw needn't show every extreme that they name: `lengths`: short proteins are more common than long ones. In every micro-batch, among proteins 4 * i to 4 * (i + 1) - 1 for each i, exactly one, at a place drawn from the seed, has length 1024.
All inputs are finite; a program needn't handle non-finite values.
Results may differ from a plain program's by a relative error of at most 0.0072.
Values may be sent and summed in bfloat16 or wider, within the bound.
No kernel may reach another device: no remote copies, remote signals or barrier semaphores. Data moves between devices by JAX's collectives and lax.ppermute only.
A program may use at most 192 MiB of HBM per device.

v0:
```python
import jax
import jax.numpy as jnp
from jax import lax
from jax.sharding import PartitionSpec as P

DILATION = 16


EPSILON = 1e-05


def padded_2(cells, sides, width):
    for axis, dim in sides:
        count = lax.axis_size(axis)
        ends = count - 1
        head = lax.slice_in_dim(cells, 0, width, axis=dim)
        tail = lax.slice_in_dim(cells, cells.shape[dim] - width, cells.shape[dim], axis=dim)
        cells = jnp.concatenate(
            [
                lax.ppermute(tail, axis, [(i, (i + 1) % count) for i in range(ends)]),
                cells,
                lax.ppermute(head, axis, [((i + 1) % count, i) for i in range(ends)]),
            ],
            axis=dim,
        )
    return cells


def layer_norm(values, norm_gain, norm_shift):
    center = values - jnp.mean(values, axis=-1, keepdims=True)
    spread = jnp.mean(center * center, axis=-1, keepdims=True)
    return center * lax.rsqrt(spread + EPSILON) * norm_gain + norm_shift


def norm_gelu(values, norm_gain, norm_shift):
    return jax.nn.gelu(layer_norm(values, norm_gain, norm_shift), approximate=False)


def contract_rows(left_side, right_side):
    return lax.dot_general(
        left_side, right_side, (((0,), (0,)), ((), ())), preferred_element_type=jnp.float32
    )


def contract_cols(left_side, right_side):
    return lax.dot_general(
        left_side, right_side, (((1,), (1,)), ((), ())), preferred_element_type=jnp.float32
    )


def fetch(params):
    (
        first_gain,
        first_shift,
        down_weight,
        down_bias,
        middle_gain,
        middle_shift,
        conv_weight,
        conv_bias,
        final_gain,
        final_shift,
        up_weight,
        up_bias,
    ) = params
    pieces = (
        lax.all_gather(down_weight, "batch", axis=1, tiled=True),
        lax.all_gather(conv_weight, "batch", axis=2, tiled=True),
        lax.all_gather(up_weight, "batch", axis=1, tiled=True),
        lax.all_gather(first_gain, "batch", axis=0, tiled=True),
        lax.all_gather(first_shift, "batch", axis=0, tiled=True),
        lax.all_gather(down_bias, "batch", axis=0, tiled=True),
        lax.all_gather(middle_gain, "batch", axis=0, tiled=True),
        lax.all_gather(middle_shift, "batch", axis=0, tiled=True),
        lax.all_gather(conv_bias, "batch", axis=0, tiled=True),
        lax.all_gather(final_gain, "batch", axis=0, tiled=True),
        lax.all_gather(final_shift, "batch", axis=0, tiled=True),
        lax.all_gather(up_bias, "batch", axis=0, tiled=True),
    )
    matrices = (
        lax.all_gather(pieces[0], "seq", axis=0, tiled=True),
        lax.all_gather(pieces[1], "seq", axis=1, tiled=True),
        lax.all_gather(pieces[2], "seq", axis=0, tiled=True),
    )
    vectors = tuple((member.astype(jnp.float32) for member in pieces[3:]))
    return (matrices, vectors)


def settle(gradients):
    pieces = (
        lax.psum_scatter(gradients[0], "batch", scatter_dimension=1, tiled=True),
        lax.psum_scatter(gradients[1], "batch", scatter_dimension=2, tiled=True),
        lax.psum_scatter(gradients[2], "batch", scatter_dimension=1, tiled=True),
        lax.psum_scatter(gradients[3], "batch", scatter_dimension=0, tiled=True),
        lax.psum_scatter(gradients[4], "batch", scatter_dimension=0, tiled=True),
        lax.psum_scatter(gradients[5], "batch", scatter_dimension=0, tiled=True),
        lax.psum_scatter(gradients[6], "batch", scatter_dimension=0, tiled=True),
        lax.psum_scatter(gradients[7], "batch", scatter_dimension=0, tiled=True),
        lax.psum_scatter(gradients[8], "batch", scatter_dimension=0, tiled=True),
        lax.psum_scatter(gradients[9], "batch", scatter_dimension=0, tiled=True),
        lax.psum_scatter(gradients[10], "batch", scatter_dimension=0, tiled=True),
        lax.psum_scatter(gradients[11], "batch", scatter_dimension=0, tiled=True),
    )
    matrices = (
        lax.psum_scatter(pieces[0], "seq", scatter_dimension=0, tiled=True),
        lax.psum_scatter(pieces[1], "seq", scatter_dimension=1, tiled=True),
        lax.psum_scatter(pieces[2], "seq", scatter_dimension=0, tiled=True),
    )
    vectors = lax.psum(
        (
            pieces[3],
            pieces[4],
            pieces[5],
            pieces[6],
            pieces[7],
            pieces[8],
            pieces[9],
            pieces[10],
            pieces[11],
        ),
        "seq",
    )
    return tuple(matrices) + tuple(vectors)


def micro_step(tokens_block, cotangent_block, length_block, position, matrices, vectors):
    down_weight, conv_weight, up_weight = matrices
    (
        first_gain,
        first_shift,
        down_bias,
        middle_gain,
        middle_shift,
        conv_bias,
        final_gain,
        final_shift,
        up_bias,
    ) = vectors
    proteins, span_len, model_width = tokens_block.shape
    inner_width = down_weight.shape[1]
    row_count = proteins * span_len
    kernel = conv_weight.shape[0]
    reach_rows = (kernel - 1) // 2 * DILATION
    inputs = tokens_block.reshape(row_count, model_width).astype(jnp.float32)
    hidden_one = norm_gelu(inputs, first_gain, first_shift).astype(jnp.bfloat16)
    narrow = jnp.dot(hidden_one, down_weight, preferred_element_type=jnp.float32) + down_bias
    valid_rows = (
        (position[None, :] < length_block[:, None]).astype(jnp.float32).reshape(row_count, 1)
    )
    conv_input = (norm_gelu(narrow, middle_gain, middle_shift) * valid_rows).astype(jnp.bfloat16)
    padded = padded_2(
        conv_input.reshape(proteins, span_len, inner_width), (("seq", 1),), reach_rows
    )
    conv_out = jnp.zeros((row_count, inner_width), jnp.float32) + conv_bias
    for tap_index in range(kernel):
        window = padded[:, tap_index * DILATION : tap_index * DILATION + span_len].reshape(
            row_count, inner_width
        )
        conv_out = conv_out + jnp.dot(
            window, conv_weight[tap_index], preferred_element_type=jnp.float32
        )
    hidden_three = norm_gelu(conv_out, final_gain, final_shift).astype(jnp.bfloat16)
    result = inputs + jnp.dot(hidden_three, up_weight, preferred_element_type=jnp.float32) + up_bias
    block_output = result.astype(jnp.bfloat16).reshape(proteins, span_len, model_width)
    incoming = cotangent_block.reshape(row_count, model_width)
    up_weight_grad = contract_rows(hidden_three, incoming)
    up_bias_grad = jnp.sum(incoming.astype(jnp.float32), axis=0)
    hidden_three_grad = contract_cols(incoming, up_weight)
    conv_out_grad, final_gain_grad, final_shift_grad = jax.vjp(
        norm_gelu, conv_out, final_gain, final_shift
    )[1](hidden_three_grad)
    conv_out_low = conv_out_grad.astype(jnp.bfloat16)
    conv_bias_grad = jnp.sum(conv_out_low.astype(jnp.float32), axis=0)
    padded_grad = padded_2(
        conv_out_low.reshape(proteins, span_len, inner_width), (("seq", 1),), reach_rows
    )
    tap_grads = []
    conv_input_grad = jnp.zeros((row_count, inner_width), jnp.float32)
    for tap_index in range(kernel):
        window = padded[:, tap_index * DILATION : tap_index * DILATION + span_len].reshape(
            row_count, inner_width
        )
        tap_grads.append(contract_rows(window, conv_out_low))
        start_row = (kernel - 1 - tap_index) * DILATION
        window_grad = padded_grad[:, start_row : start_row + span_len].reshape(
            row_count, inner_width
        )
        conv_input_grad = conv_input_grad + contract_cols(window_grad, conv_weight[tap_index])
    conv_weight_grad = jnp.stack(tap_grads)
    conv_input_grad = conv_input_grad * valid_rows
    narrow_grad, middle_gain_grad, middle_shift_grad = jax.vjp(
        norm_gelu, narrow, middle_gain, middle_shift
    )[1](conv_input_grad)
    narrow_low = narrow_grad.astype(jnp.bfloat16)
    down_bias_grad = jnp.sum(narrow_low.astype(jnp.float32), axis=0)
    down_weight_grad = contract_rows(hidden_one, narrow_low)
    hidden_one_grad = contract_cols(narrow_low, down_weight)
    inputs_grad, first_gain_grad, first_shift_grad = jax.vjp(
        norm_gelu, inputs, first_gain, first_shift
    )[1](hidden_one_grad)
    tokens_grad = (
        (inputs_grad + incoming.astype(jnp.float32))
        .astype(jnp.bfloat16)
        .reshape(proteins, span_len, model_width)
    )
    gradients = (
        down_weight_grad,
        conv_weight_grad,
        up_weight_grad,
        first_gain_grad,
        first_shift_grad,
        down_bias_grad,
        middle_gain_grad,
        middle_shift_grad,
        conv_bias_grad,
        final_gain_grad,
        final_shift_grad,
        up_bias_grad,
    )
    return (block_output, tokens_grad, gradients)


def body(
    tokens,
    lengths,
    first_gain,
    first_shift,
    down_weight,
    down_bias,
    middle_gain,
    middle_shift,
    conv_weight,
    conv_bias,
    final_gain,
    final_shift,
    up_weight,
    up_bias,
    cotangent,
):
    params = (
        first_gain,
        first_shift,
        down_weight,
        down_bias,
        middle_gain,
        middle_shift,
        conv_weight,
        conv_bias,
        final_gain,
        final_shift,
        up_weight,
        up_bias,
    )
    micro_count = tokens.shape[0]
    span_len = tokens.shape[2]
    position = lax.axis_index("seq") * span_len + jnp.arange(span_len, dtype=jnp.int32)
    output_list = []
    input_grad_list = []
    totals = None
    for micro_index in range(micro_count):
        matrices, vectors = fetch(params)
        block_output, tokens_grad, gradients = micro_step(
            tokens[micro_index],
            cotangent[micro_index],
            lengths[micro_index],
            position,
            matrices,
            vectors,
        )
        output_list.append(block_output)
        input_grad_list.append(tokens_grad)
        gradients = settle(gradients)
        if totals is None:
            totals = gradients
        else:
            totals = tuple(
                (first_term + second_term for first_term, second_term in zip(totals, gradients))
            )
    return (
        jnp.stack(output_list),
        jnp.stack(input_grad_list),
        totals[3],
        totals[4],
        totals[0],
        totals[5],
        totals[6],
        totals[7],
        totals[1],
        totals[8],
        totals[9],
        totals[10],
        totals[2],
        totals[11],
    )


def solution(mesh):
    return jax.shard_map(
        body,
        mesh=mesh,
        in_specs=(
            P(None, "batch", "seq", None),
            P(None, "batch"),
            P("batch"),
            P("batch"),
            P("seq", "batch"),
            P("batch"),
            P("batch"),
            P("batch"),
            P(None, "seq", "batch"),
            P("batch"),
            P("batch"),
            P("batch"),
            P("seq", "batch"),
            P("batch"),
            P(None, "batch", "seq", None),
        ),
        out_specs=(
            P(None, "batch", "seq", None),
            P(None, "batch", "seq", None),
            P("batch"),
            P("batch"),
            P("seq", "batch"),
            P("batch"),
            P("batch"),
            P("batch"),
            P(None, "seq", "batch"),
            P("batch"),
            P("batch"),
            P("batch"),
            P("seq", "batch"),
            P("batch"),
        ),
        check_vma=False,
    )
```

profile of v0, /device:TPU:0, one launch (start us, length us, event | category | flops | bytes accessed | tf_op | source)
XLA Modules:
  0.0 574.9 jit_solution(4036589247653241440)
XLA Ops:
  7.2 16.7 %all_gather.63 = bf16[320,640]{0,1:T(8,128)(2,1)S(1)} all-gather(bf16[320,80]{0,1:T(8,128)(2,1)} %param.19), channel_id=1, replica_groups=mesh['seq'=4,'batch'=8] {'batch'}, dimensions={1}, use_global_device_ids=true | all-gather | bytes 460800 | tf_op jit(solution)/shard_map/all_gather | solution.py:67
  26.2 27.0 %all_gather.68 = bf16[5,160,640]{1,0,2:T(8,128)(2,1)S(1)} all-gather(bf16[5,160,80]{1,0,2:T(8,128)(2,1)S(1)} %copy.40), channel_id=1, replica_groups=mesh['seq'=4,'batch'=8] {'batch'}, dimensions={2}, use_global_device_ids=true | all-gather | bytes 1152000 | tf_op jit(solution)/shard_map/all_gather | solution.py:68
  56.2 15.6 %all_gather.72 = bf16[160,1280]{0,1:T(8,128)(2,1)S(1)} all-gather(bf16[160,160]{0,1:T(8,128)(2,1)S(1)} %copy.42), channel_id=1, replica_groups=mesh['seq'=4,'batch'=8] {'batch'}, dimensions={1}, use_global_device_ids=true | all-gather | bytes 460800 | tf_op jit(solution)/shard_map/all_gather | solution.py:69
  77.0 30.4 %all-reduce.20 = (bf16[1280]{0:T(1024)(128)(2,1)S(1)}, bf16[1280]{0:T(1024)(128)(2,1)S(1)}, bf16[640]{0:T(1024)(128)(2,1)S(1)}, bf16[640]{0:T(1024)(128)(2,1)S(1...) all-reduce(bf16[1280]{0:T(1024)(128)(2,1)S(1)} %dynamic-update-slic, ...), channel_id=1, replica_groups=mesh['seq'=4,'batch'=8] {'batch'}, use_global_device_ids=true, to_apply=%add.2 | all-reduce | flops 7680 | bytes 30720
  119.5 27.4 %multiply_convert_fusion = (bf16[1024,1280]{1,0:T(8,128)(2,1)S(1)}, f32[1024,1280]{1,0:T(8,128)}, bf16[1024,1280]{1,0:T(8,128)(2,1)}, f32[1024,1280]{1,0:T(8,128)}) fusion(f32[1024]{0:T(1024)S(1)} %rsqrt.69, f32[1024]{0:T(1024)S(1)} %bitcast.317, f32[1280]{0:T(1024)S(1)} %convert_element_type.149, f32[1280]{0:T(1024)S(1)} %convert_element_type.148, ...), kind=kLoop, calls=%fused_computation.52 | loop fusion | flops 183500800 | bytes 20998144 | tf_op jit(solution)/shard_map/convert_element_type | solution.py:145
  156.0 7.1 %multiply_convert_fusion.3 = bf16[1024,640]{1,0:T(8,128)(2,1)S(1)} fusion(f32[1024]{0:T(1024)S(1)} %bitcast.326, f32[1024]{0:T(1024)S(1)} %fusion.92, f32[640]{0:T(1024)S(1)} %convert_element_type.153, f32[640]{0:T(1024)S(1)} %convert_element_type.152, f32[1024]{0:T(1024)S(1)} %broadcast_multiply_fusion.1, f32[1024,640]{1,0:T(8,128)S(1)} %fusion.117, ...), kind=kLoop, calls=%fused_computation.128 | loop fusion | flops 46530560 | bytes 3952128 | tf_op jit(solution)/shard_map/convert_element_type | solution.py:150
  184.7 11.5 %multiply_reduce_fusion = (f32[640]{0:T(1024)}, f32[1024]{0:T(1024)S(1)}, f32[640]{0:T(1024)}, f32[1024,640]{1,0:T(8,128)S(1)}, f32[1024,640]{1,0:T(8,128)S(1)}) fusion(f32[1024,640]{1,0:T(8,128)S(1)} %get-tuple-element.212, f32[1024]{0:T(1024)S(1)} %fusion.93, f32[1024]{0:T(1024)S(1)} %broadcast_multiply_fusion, f32[640]{0:T(1024)S(1)} %convert_element_type.157, ...), kind=kOutput, calls=%fused_computation.92 | convolution fusion | flops 1730803456 | bytes 12146688 | tf_op jit(solution)/shard_map/dot_general | solution.py:46
  214.2 9.4 %fusion.98 = (f32[640]{0:T(1024)}, f32[1024]{0:T(1024)S(1)}, f32[1024]{0:T(1024)S(1)}, f32[1024,640]{1,0:T(8,128)S(1)}) fusion(f32[640]{0:T(1024)S(1)} %convert_element_type.152, f32[1024]{0:T(1024)S(1)} %broadcast_multiply_fusion.1, f32[1024,640]{1,0:T(8,128)S(1)} %copy-done.2, f32[640]{0:T(1024)S(1)} %convert_element_type.151, ...), kind=kOutput, calls=%fused_computation.282 | convolution fusion | flops 897185152 | bytes 20519424 | tf_op jit(solution)/shard_map/dot_general | solution.py:46
  223.7 7.1 %multiply_convert_fusion.5 = bf16[1024,640]{1,0:T(8,128)(2,1)S(1)} fusion(f32[1024]{0:T(1024)S(1)} %bitcast.324, f32[640]{0:T(1024)S(1)} %convert_element_type.153, f32[640]{0:T(1024)S(1)} %convert_element_type.152, f32[1024]{0:T(1024)S(1)} %fusion.90, f32[1024]{0:T(1024)S(1)} %broadcast_multiply_fusion.3, f32[1024,640]{1,0:T(8,128)S(1)} %copy-done, ...), kind=kLoop, calls=%fused_computation.159 | loop fusion | flops 46530560 | bytes 3952128 | tf_op jit(solution)/shard_map/convert_element_type | solution.py:150
  238.5 5.8 %collective-permute-done.1 = bf16[4,32,640]{2,1,0:T(8,128)(2,1)S(1)} collective-permute-done((bf16[4,32,640]{2,1,0:T(8,128)(2,1)S(1)}, bf16[4,32,640]{2,1,0:T(8,128)(2,1)S(1)}, u32[]{:S(2)}, u32[]{:S(2)}) %collective-permute-start.1) | collective-permute-done | bytes 163872 | tf_op jit(solution)/shard_map/ppermute | solution.py:22
  252.5 9.1 %multiply_reduce_fusion.1 = (f32[640]{0:T(1024)S(1)}, f32[1024]{0:T(1024)S(1)}, f32[640]{0:T(1024)S(1)}, f32[1024,640]{1,0:T(8,128)S(1)}, f32[1024,640]{1,0:T(8,128)S(1)}) fusion(f32[1024,640]{1,0:T(8,128)S(1)} %get-tuple-element.215, f32[1024]{0:T(1024)S(1)} %fusion.91, f32[1024]{0:T(1024)S(1)} %broadcast_multiply_fusion.2, ...), kind=kOutput, calls=%fused_computation.93 | convolution fusion | flops 1730803456 | bytes 12146688 | tf_op jit(solution)/shard_map/dot_general | solution.py:46
  265.5 5.5 collective-permute-start.5
  280.0 11.0 %fusion.99 = (f32[640]{0:T(1024)S(1)}, f32[1024]{0:T(1024)S(1)}, f32[1024]{0:T(1024)S(1)}, f32[640]{0:T(1024)S(1)}, f32[1024,640]{1,0:T(8,128)S(1)}) fusion(f32[640]{0:T(1024)S(1)} %convert_element_type.152, f32[1024]{0:T(1024)S(1)} %broadcast_multiply_fusion.3, f32[1024,640]{1,0:T(8,128)S(1)} %copy-done, f32[640]{0:T(1024)S(1)} %convert_element_type.151, ...), kind=kOutput, calls=%fused_computation.283 | convolution fusion | flops 901772032 | bytes 23151616 | tf_op jit(solution)/shard_map/dot_general | solution.py:46
  330.8 8.0 %add.455 = f32[5,640,640]{2,1,0:T(8,128)} add(f32[5,640,640]{2,1,0:T(8,128)} %bitcast_dynamic-update-slice_fusion.5, f32[5,640,640]{2,1,0:T(8,128)S(1)} %bitcast_dynamic-update-slice_fusion) | non-fusion elementwise | flops 2048000 | bytes 24576000 | tf_op jit(solution)/shard_map/add | solution.py:277
  338.7 13.4 %copy.49 = f32[5,640,640]{1,0,2:T(8,128)} copy(f32[5,640,640]{2,1,0:T(8,128)} %add.455) | data formatting | bytes 16384000
  352.2 9.7 %copy.57 = f32[80,8,5,640]{3,1,2,0:T(8,128)} copy(f32[80,8,5,640]{3,2,1,0:T(8,128)} %bitcast.267) | data formatting | bytes 16384000
  384.7 15.5 %fusion.26 = (f32[1280]{0:T(1024)S(1)}, f32[1024]{0:T(1024)S(1)}, f32[1024]{0:T(1024)S(1)}, f32[1280]{0:T(1024)S(1)}, f32[1280]{0:T(1024)S(1)}, /*index=5*/f32[1...) fusion(f32[1024]{0:T(1024)S(1)} %copy-done.50, f32[1024]{0:T(1024)S(1)} %bitcast.315, ...), kind=kOutput, calls=%fused_computation.40 | convolution fusion | flops 1740628992 | bytes 34461696 | tf_op jit(solution)/shard_map/dot_general | solution.py:46
  402.5 9.8 %fusion.100 = (f32[1024]{0:T(1024)S(1)}, f32[1024,1280]{1,0:T(8,128)}, f32[1024]{0:T(1024)S(1)}, f32[1024,1280]{1,0:T(8,128)}) fusion(f32[1024]{0:T(1024)S(1)} %multiply_multiply_fusion.33, f32[1024]{0:T(1024)S(1)} %bitcast.316, bf16[2,4,256,1280]{3,2,1,0:T(8,128)(2,1)} %param.15, f32[1024]{0:T(1024)S(1)} %copy-done.50, ...), kind=kLoop, calls=%fused_computation.284 | loop fusion | flops 20969472 | bytes 26252288 | tf_op jit(solution)/shard_map/transpose(jvp())/reduce_sum | solution.py:30
  412.3 28.9 %all-reduce.18 = (f32[1280]{0:T(1024)S(1)}, f32[1280]{0:T(1024)S(1)}, f32[640]{0:T(1024)S(1)}, f32[640]{0:T(1024)S(1)}, f32[640]{0:T(1024)S(1)}, /*index=5*/f32[...) all-reduce(f32[1280]{0:T(1024)S(1)} %add.442, ...), channel_id=17, replica_groups=mesh['seq'=4,'batch'=8] {'batch'}, use_global_device_ids=true, to_apply=%region_25.0.clone | all-reduce | flops 7680 | bytes 61440
  441.9 11.8 %all-reduce.19 = (f32[160]{0:T(256)}, f32[160]{0:T(256)}, f32[80]{0:T(128)}, f32[80]{0:T(128)}, f32[80]{0:T(128)}, /*index=5*/f32[80]{0:T(128)}, f32[80]{0:T(128)}, f32[80]{0:T(128)}, f32[160]{0:T(256)}) all-reduce(f32[160]{0:T(256)S(1)} %dynamic-slice.10, f32[160]{0:T(256)S(1)} %dynamic-slice.12, ...), channel_id=1, replica_groups=mesh['seq'=4,'batch'=8] {'seq'}, use_global_device_ids=true, to_apply=%region_26.0 | all-reduce | flops 960 | bytes 7680 | tf_op jit(solution)/shard_map/psum | solution.py:109
  453.7 23.4 %reduce-scatter.23.cloned.1.call-done = f32[80,3200]{1,0:T(8,128)} async-done(((f32[640,3200]{1,0:T(8,128)}), f32[80,3200]{1,0:T(8,128)}) %reduce-scatter.23.cloned.1.call-update) | async-done | bytes 1024016
  489.5 14.5 %reduce-scatter.19.cloned.1.call-done = f32[320,80]{1,0:T(8,128)} async-done(((f32[1280,80]{1,0:T(8,128)}), f32[320,80]{1,0:T(8,128)}) %reduce-scatter.19.cloned.1.call-update) | async-done | bytes 102416
  505.7 27.2 %reduce-scatter.21.cloned.1.call-done = f32[160,160]{1,0:T(8,128)} async-done(((f32[640,160]{1,0:T(8,128)}), f32[160,160]{1,0:T(8,128)}) %reduce-scatter.21.cloned.1.call-update) | async-done | bytes 102416
  532.9 35.3 %reduce-scatter.13.cloned.1.call-done = f32[5,160,80]{2,1,0:T(8,128)} async-done(((f32[5,640,80]{2,1,0:T(8,128)}), f32[5,160,80]{2,1,0:T(8,128)}) %reduce-scatter.13.cloned.1.call-update) | async-done | bytes 256016 | tf_op jit(solution)/shard_map/reduce_scatter | solution.py:106
  (363 shorter events, 175.6 us)
Async XLA Ops:
  7.2 139.8 %all-gather.4.cloned.1.call-start = ((), (), s32[]{:S(2)}) async-start(), calls=%async_computation.6 | async-start | bytes 2048000 | tf_op jit(solution)/shard_map/all_gather | solution.py:81
  24.9 150.8 %all-gather.6.cloned.1.call-start = ((), (), s32[]{:S(2)}) async-start(), calls=%async_computation.7 | async-start | bytes 5120000 | tf_op jit(solution)/shard_map/all_gather | solution.py:82
  55.9 19.6 %copy-start.73 = (bf16[80]{0:T(256)(128)(2,1)S(1)}, bf16[80]{0:T(256)(128)(2,1)}, u32[]{:S(2)}) copy-start(bf16[80]{0:T(256)(128)(2,1)} %param.22) | copy-start | bytes 484
  55.9 19.8 %copy-start.74 = (bf16[80]{0:T(256)(128)(2,1)S(1)}, bf16[80]{0:T(256)(128)(2,1)}, u32[]{:S(2)}) copy-start(bf16[80]{0:T(256)(128)(2,1)} %param.20) | copy-start | bytes 484
  56.0 20.0 %copy-start.75 = (bf16[80]{0:T(256)(128)(2,1)S(1)}, bf16[80]{0:T(256)(128)(2,1)}, u32[]{:S(2)}) copy-start(bf16[80]{0:T(256)(128)(2,1)} %param.25) | copy-start | bytes 484
  56.0 20.3 %copy-start.76 = (bf16[160]{0:T(256)(128)(2,1)S(1)}, bf16[160]{0:T(256)(128)(2,1)}, u32[]{:S(2)}) copy-start(bf16[160]{0:T(256)(128)(2,1)} %param.17) | copy-start | bytes 964
  56.0 20.5 %copy-start.77 = (bf16[160]{0:T(256)(128)(2,1)S(1)}, bf16[160]{0:T(256)(128)(2,1)}, u32[]{:S(2)}) copy-start(bf16[160]{0:T(256)(128)(2,1)} %param.18) | copy-start | bytes 964
  56.0 20.7 %copy-start.78 = (bf16[160]{0:T(256)(128)(2,1)S(1)}, bf16[160]{0:T(256)(128)(2,1)}, u32[]{:S(2)}) copy-start(bf16[160]{0:T(256)(128)(2,1)} %param.28) | copy-start | bytes 964
  56.0 128.7 %all-gather.8.cloned.1.call-start = ((), (), s32[]{:S(2)}) async-start(), calls=%async_computation.8 | async-start | bytes 2048000 | tf_op jit(solution)/shard_map/all_gather | solution.py:83
  72.8 42.3 %slice-start.2 = ((s8[5242880]{0:T(1024)(128)(4,1)}), s8[1048576]{0:T(1024)(128)(4,1)S(1)}, s32[]{:S(2)}) async-start(s8[5242880]{0:T(1024)(128)(4,1)} %bitcast.269), calls=%async_computation.17 | async-start | bytes 2097152
  72.8 309.5 %reduce-scatter.15.cloned.1.call-start = ((), (), s32[]{:S(2)}) async-start(), calls=%async_computation.10 | async-start | bytes 3686400 | tf_op jit(solution)/shard_map/reduce_scatter | solution.py:91
  163.2 6.2 %collective-permute-start.2 = (bf16[4,32,640]{2,1,0:T(8,128)(2,1)S(1)}, bf16[4,32,640]{2,1,0:T(8,128)(2,1)S(1)}, u32[]{:S(2)}, u32[]{:S(2)}) collective-permute-start(bf16[4,32,640]{2,1,0:T(8,128)(2,1)S(1)} %get-tuple-element.196), channel_id=1, source_target_pairs={{0,8},{8,16},{16,24},{1,9},{9,17},{17,25},{2,10},{10,18},{18,26},{... | collective-permute-start | bytes 491528 | tf_op jit(solution)/shard_map/ppermute | solution.py:20
  166.6 7.2 %collective-permute-start.3 = (bf16[4,32,640]{2,1,0:T(8,128)(2,1)S(1)}, bf16[4,32,640]{2,1,0:T(8,128)(2,1)S(1)}, u32[]{:S(2)}, u32[]{:S(2)}) collective-permute-start(bf16[4,32,640]{2,1,0:T(8,128)(2,1)S(1)} %get-tuple-element.197), channel_id=1, source_target_pairs={{8,0},{16,8},{24,16},{9,1},{17,9},{25,17},{10,2},{18,10},{26,18},{... | collective-permute-start | bytes 491528 | tf_op jit(solution)/shard_map/ppermute | solution.py:22
  199.5 8.6 %collective-permute-start.6 = (bf16[4,32,640]{2,1,0:T(8,128)(2,1)S(1)}, bf16[4,32,640]{2,1,0:T(8,128)(2,1)S(1)}, u32[]{:S(2)}, u32[]{:S(2)}) collective-permute-start(bf16[4,32,640]{2,1,0:T(8,128)(2,1)S(1)} %get-tuple-element.192), channel_id=1, source_target_pairs={{8,0},{16,8},{24,16},{9,1},{17,9},{25,17},{10,2},{18,10},{26,18},{... | collective-permute-start | bytes 491528 | tf_op jit(solution)/shard_map/ppermute | solution.py:22
  201.4 7.7 %collective-permute-start.7 = (bf16[4,32,640]{2,1,0:T(8,128)(2,1)S(1)}, bf16[4,32,640]{2,1,0:T(8,128)(2,1)S(1)}, u32[]{:S(2)}, u32[]{:S(2)}) collective-permute-start(bf16[4,32,640]{2,1,0:T(8,128)(2,1)S(1)} %get-tuple-element.193), channel_id=1, source_target_pairs={{0,8},{8,16},{16,24},{1,9},{9,17},{17,25},{2,10},{10,18},{18,26},{... | collective-permute-start | bytes 491528 | tf_op jit(solution)/shard_map/ppermute | solution.py:20
  230.8 7.7 %collective-permute-start = (bf16[4,32,640]{2,1,0:T(8,128)(2,1)S(1)}, bf16[4,32,640]{2,1,0:T(8,128)(2,1)S(1)}, u32[]{:S(2)}, u32[]{:S(2)}) collective-permute-start(bf16[4,32,640]{2,1,0:T(8,128)(2,1)S(1)} %get-tuple-element.188), channel_id=1, source_target_pairs={{0,8},{8,16},{16,24},{1,9},{9,17},{17,25},{2,10},{10,18},{18,26},{... | collective-permute-start | bytes 491528 | tf_op jit(solution)/shard_map/ppermute | solution.py:20
  235.7 8.6 %collective-permute-start.1 = (bf16[4,32,640]{2,1,0:T(8,128)(2,1)S(1)}, bf16[4,32,640]{2,1,0:T(8,128)(2,1)S(1)}, u32[]{:S(2)}, u32[]{:S(2)}) collective-permute-start(bf16[4,32,640]{2,1,0:T(8,128)(2,1)S(1)} %get-tuple-element.189), channel_id=1, source_target_pairs={{8,0},{16,8},{24,16},{9,1},{17,9},{25,17},{10,2},{18,10},{26,18},{... | collective-permute-start | bytes 491528 | tf_op jit(solution)/shard_map/ppermute | solution.py:22
  264.2 8.1 %collective-permute-start.4 = (bf16[4,32,640]{2,1,0:T(8,128)(2,1)S(1)}, bf16[4,32,640]{2,1,0:T(8,128)(2,1)S(1)}, u32[]{:S(2)}, u32[]{:S(2)}) collective-permute-start(bf16[4,32,640]{2,1,0:T(8,128)(2,1)S(1)} %get-tuple-element.184), channel_id=1, source_target_pairs={{8,0},{16,8},{24,16},{9,1},{17,9},{25,17},{10,2},{18,10},{26,18},{... | collective-permute-start | bytes 491528 | tf_op jit(solution)/shard_map/ppermute | solution.py:22
  265.5 8.3 %collective-permute-start.5 = (bf16[4,32,640]{2,1,0:T(8,128)(2,1)S(1)}, bf16[4,32,640]{2,1,0:T(8,128)(2,1)S(1)}, u32[]{:S(2)}, u32[]{:S(2)}) collective-permute-start(bf16[4,32,640]{2,1,0:T(8,128)(2,1)S(1)} %get-tuple-element.185), channel_id=1, source_target_pairs={{0,8},{8,16},{16,24},{1,9},{9,17},{17,25},{2,10},{10,18},{18,26},{... | collective-permute-start | bytes 491528 | tf_op jit(solution)/shard_map/ppermute | solution.py:20
  301.7 98.6 %reduce-scatter.17.cloned.1.call-start = ((), (), s32[]{:S(2)}) async-start(), calls=%async_computation.11 | async-start | bytes 3686400 | tf_op jit(solution)/shard_map/reduce_scatter | solution.py:93
  309.5 167.6 %reduce-scatter.23.cloned.1.call-start = ((), (), s32[]{:S(2)}) async-start(), calls=%async_computation.14 | async-start | bytes 9216000
  361.9 142.1 %reduce-scatter.19.cloned.1.call-start = ((), (), s32[]{:S(2)}) async-start(), calls=%async_computation.12 | async-start | bytes 819200
  384.4 148.5 %reduce-scatter.21.cloned.1.call-start = ((), (), s32[]{:S(2)}) async-start(), calls=%async_computation.13 | async-start | bytes 819200
  402.4 165.8 %reduce-scatter.13.cloned.1.call-start = ((), (), s32[]{:S(2)}) async-start(), calls=%async_computation.9 | async-start | bytes 2048000 | tf_op jit(solution)/shard_map/reduce_scatter | solution.py:106
  (78 other events, 427.7 us)
Sparse Core Ops, SparseCore 0:
  25.0 32.6 all-gather.3
  59.5 51.8 all-gather.5
  113.3 31.5 all-gather.7
  301.9 42.7 reduce-scatter.14
  346.9 40.1 reduce-scatter.16
  389.3 87.7 reduce-scatter.22
  480.2 23.7 reduce-scatter.18
  507.5 25.3 reduce-scatter.20
  536.8 31.3 reduce-scatter.12
where the time goes:
time: 581 us; the launch traced here: 575 us
  matrix products  135 us (23%)
  blocking collectives  130 us (22%)
  waiting for transfers between devices  115 us (20%)
  other arithmetic  95.4 us (16%)
  local copies, waits for them, and re-layouts  55.5 us (10%)
  starting transfers between devices  25.2 us (4%)
  between operations  18.2 us (3%)
    dot_general x14, matrix products, contract_cols(): lax.dot_general(left_side, right_side, (((1,), (1,)), ((), ())), preferre...  73.3 us
    unnamed x12, waiting for transfers between devices  65.3 us
    unnamed x2, blocking collectives  59.2 us
    unnamed x213, local copies, waits for them, and re-layouts  44.6 us
    reduce_scatter x1, waiting for transfers between devices, settle(): lax.psum_scatter(pieces[1], 'seq', scatter_dimension=1, tiled=True)  35.3 us
    dot_general x14, matrix products, contract_rows(): lax.dot_general(left_side, right_side, (((0,), (0,)), ((), ())), preferre...  33.5 us
    convert_element_type x1, other arithmetic, micro_step(): hidden_one = norm_gelu(inputs, first_gain, first_shift).astype(jnp.bfloat16)  27.4 us
    all_gather x1, blocking collectives, fetch(): lax.all_gather(conv_weight, 'batch', axis=2, tiled=True)  27 us
  transfers between devices with their start and end apart: 17, of which 11 were waited for; matrix products, arithmetic and copies ran while one was open for 34% of the time, Pallas kernels for 0%

commit v1 on v0

v1 whole, which is shorter than its diff:
```python
import functools
import math

import jax
import jax.numpy as jnp
from jax import lax
from jax.experimental import pallas as pl
from jax.experimental.pallas import tpu as pltpu
from jax.sharding import PartitionSpec as P

DILATION = 16
EPSILON = 1e-05
BF = jnp.bfloat16
F32 = jnp.float32
ROOT_HALF = 0.7071067811865476
PHI_SCALE = 0.3989422804014327
MIB = 1 << 20

WIDE = ("first_gain", "first_shift", "up_bias")
NARROW = ("down_bias", "middle_gain", "middle_shift", "conv_bias", "final_gain", "final_shift")
ROW = {name: row for row, name in enumerate(WIDE + NARROW)}
TABLE_ROWS = 16


class Grid:
    def __init__(self, seq, batch):
        self.seq, self.batch = seq, batch
        self.side = math.isqrt(seq)
        assert self.side * self.side == seq
        self.depth = batch // 2

    def here(self):
        s, b = lax.axis_index("seq"), lax.axis_index("batch")
        return s // self.side, s % self.side, b // 2, b % 2

    def send(self, value, move):
        pairs = []
        for s in range(self.seq):
            for b in range(self.batch):
                h, l, z, c = move(s // self.side, s % self.side, b // 2, b % 2)
                pairs.append((s * self.batch + b, (h * self.side + l) * self.batch + z * 2 + c))
        return lax.ppermute(value, ("seq", "batch"), pairs)

    def high(self, value, k):
        return self.send(value, lambda h, l, z, c: ((h + k) % self.side, l, z, c))

    def low(self, value, k):
        return self.send(value, lambda h, l, z, c: (h, (l + k) % self.side, z, c))

    def deep(self, value, k):
        return self.send(value, lambda h, l, z, c: (h, l, (z + k) % self.depth, c))

    def core(self, value):
        return self.send(value, lambda h, l, z, c: (h, l, z, 1 - c))

    def gather(self, piece):
        side, half = self.side, self.depth // 2
        column = jnp.stack([piece] + [self.deep(piece, k) for k in range(1, self.depth)])
        one, two = column[:half], column[half:]
        one = jnp.stack([one] + [self.low(one, k) for k in range(1, side)])
        two = jnp.stack([two] + [self.high(two, k) for k in range(1, side)])
        one = jnp.stack([one] + [self.high(one, k) for k in range(1, side)])
        two = jnp.stack([two] + [self.low(two, k) for k in range(1, side)], axis=1)
        mine = jnp.concatenate([one, two], axis=2)
        other = self.core(mine)
        return jnp.stack([mine, other])

    def scatter(self, pieces):
        side, half = self.side, self.depth // 2

        def add(terms, kind):
            total = terms[0].astype(F32)
            for term in terms[1:]:
                total = total + term.astype(F32)
            return total.astype(kind)

        total = add([pieces[0], self.core(pieces[1])], BF)
        one, two = total[:, :, :half], total[:, :, half:]
        one = add([one[0]] + [self.high(one[k], -k) for k in range(1, side)], BF)
        two = add([two[:, 0]] + [self.low(two[:, k], -k) for k in range(1, side)], BF)
        one = add([one[0]] + [self.low(one[k], -k) for k in range(1, side)], BF)
        two = add([two[0]] + [self.high(two[k], -k) for k in range(1, side)], BF)
        column = jnp.concatenate([one, two], axis=0)
        return add([column[0]] + [self.deep(column[k], -k) for k in range(1, self.depth)], F32)


def distance(grid, place, s, b):
    side, depth = grid.side, grid.depth
    h, l, z, c = place[0], place[1], place[2], place[3]
    rh = lax.rem(h - s // side + side, side)
    rl = lax.rem(l - s % side + side, side)
    rz = lax.rem(z - b // 2 + depth, depth)
    core = b - (b // 2) * 2
    rc = jnp.where(core == c, 0, 1)
    return ((rc * side + rh) * side + rl) * depth + rz


def normed(values):
    center = values - jnp.mean(values, axis=-1, keepdims=True)
    spread = jnp.mean(center * center, axis=-1, keepdims=True)
    inverse = lax.rsqrt(spread + EPSILON)
    return center * inverse, inverse


def cumulative(s):
    return 0.5 + 0.5 * lax.erf(s * ROOT_HALF)


def gelu(s):
    return s * cumulative(s)


def gelu_slope(s):
    return cumulative(s) + s * (PHI_SCALE * jnp.exp(-0.5 * s * s))


def back_rows(q, gain, unit, inverse):
    weighted = q * gain
    first = jnp.mean(weighted, axis=-1, keepdims=True)
    second = jnp.mean(weighted * unit, axis=-1, keepdims=True)
    return (weighted - first - unit * second) * inverse


def row_sum(values):
    return jnp.sum(values, axis=0, keepdims=True)


def dot_nn(left, right):
    return lax.dot_general(left, right, (((1,), (0,)), ((), ())), preferred_element_type=F32)


def dot_nt(left, right):
    return lax.dot_general(left, right, (((1,), (1,)), ((), ())), preferred_element_type=F32)


def dot_tn(left, right):
    return lax.dot_general(left, right, (((0,), (0,)), ((), ())), preferred_element_type=F32)


def params(limit):
    return pltpu.CompilerParams(
        dimension_semantics=("arbitrary",), vmem_limit_bytes=limit * MIB
    )


def cost(flops, bytes_accessed, transcendentals=0):
    return pl.CostEstimate(
        flops=flops, bytes_accessed=bytes_accessed, transcendentals=transcendentals
    )


def whole(shape):
    return pl.BlockSpec(shape, lambda i, *_: (0,) * len(shape))


def rows_of(block):
    return pl.BlockSpec(block, lambda i, *_: (i,) + (0,) * (len(block) - 1))


def sds(shape, kind):
    return jax.ShapeDtypeStruct(shape, kind)


def assemble_down_kernel(grid, hb, dl, place, pieces, down_ref, table_ref):
    wide = down_ref.shape[2] // grid.batch
    hidden = hb * grid.batch
    table_ref[...] = jnp.zeros_like(table_ref)
    for b in range(grid.batch):
        for s in range(grid.seq):
            down_ref[b, :, s * dl : (s + 1) * dl] = pieces[distance(grid, place, s, b), 0:hb, :]
        vec = pieces[distance(grid, place, 0, b), hb : hb + 16, :].astype(F32)
        at = 0
        for name in WIDE + NARROW:
            width = wide if name in WIDE else hidden // grid.batch
            done = 0
            while done < width:
                line, col = at // dl, at % dl
                take = min(width - done, dl - col)
                start = b * width + done
                table_ref[ROW[name] : ROW[name] + 1, start : start + take] = vec[
                    line : line + 1, col : col + take
                ]
                at += take
                done += take


def assemble_down(grid, hb, model, pieces, place):
    dl = model // grid.seq
    count = grid.seq * grid.batch
    return pl.pallas_call(
        functools.partial(assemble_down_kernel, grid, hb, dl),
        out_shape=(sds((grid.batch, hb, model), BF), sds((TABLE_ROWS, model), F32)),
        grid_spec=pltpu.PrefetchScalarGridSpec(
            num_scalar_prefetch=1,
            grid=(1,),
            in_specs=[whole(pieces.shape)],
            out_specs=[whole((grid.batch, hb, model)), whole((TABLE_ROWS, model))],
        ),
        compiler_params=params(32),
        cost_estimate=cost(0, 4 * count * hb * dl),
        name="assemble_down",
    )(place, pieces)


def assemble_rest_kernel(grid, hb, hl, taps, fold, place, pieces, conv_ref, up_ref):
    def block(b, _):
        for s in range(grid.seq):
            at = distance(grid, place, s, b)
            piece = pieces[at]
            for k in range(taps):
                conv_ref[k, b, :, s * hl : (s + 1) * hl] = piece[:, k * hl : (k + 1) * hl]
            for f in range(fold):
                col = (taps + f) * hl
                up_ref[b, f, :, s * hl : (s + 1) * hl] = piece[:, col : col + hl]
        return 0

    lax.fori_loop(0, grid.batch, block, 0)


def assemble_rest(grid, hb, hidden, taps, fold, pieces, place):
    hl = hidden // grid.seq
    return pl.pallas_call(
        functools.partial(assemble_rest_kernel, grid, hb, hl, taps, fold),
        out_shape=(
            sds((taps, grid.batch, hb, hidden), BF),
            sds((grid.batch, fold, hb, hidden), BF),
        ),
        grid_spec=pltpu.PrefetchScalarGridSpec(
            num_scalar_prefetch=1,
            grid=(1,),
            in_specs=[whole(pieces.shape)],
            out_specs=[
                whole((taps, grid.batch, hb, hidden)),
                whole((grid.batch, fold, hb, hidden)),
            ],
        ),
        compiler_params=params(48),
        cost_estimate=cost(0, 4 * (taps + fold) * hidden * hidden),
        name="assemble_rest",
    )(place, pieces)


def stage_one_kernel(
    start_ref, length_ref, tokens, table, down_t, hidden_one, narrow, conv_input
):
    model = tokens.shape[2]
    hidden = narrow.shape[2]

    def vec(name, width):
        return table[ROW[name] : ROW[name] + 1, 0:width]

    unit, _ = normed(tokens[0].astype(F32))
    one = gelu(unit * vec("first_gain", model) + vec("first_shift", model)).astype(BF)
    hidden_one[0] = one
    values = dot_nt(one, down_t[...]) + vec("down_bias", hidden)
    narrow[0] = values
    unit, _ = normed(values)
    active = gelu(unit * vec("middle_gain", hidden) + vec("middle_shift", hidden))
    rows = values.shape[0]
    position = start_ref[0] + lax.broadcasted_iota(jnp.int32, (rows, 1), 0)
    valid = (position < length_ref[pl.program_id(0)]).astype(F32)
    conv_input[0] = (active * valid).astype(BF)


def stage_one(tokens, table, down_t, start, lengths):
    count, span, model = tokens.shape
    hidden = down_t.shape[0]
    return pl.pallas_call(
        stage_one_kernel,
        out_shape=(
            sds((count, span, model), BF),
            sds((count, span, hidden), F32),
            sds((count, span, hidden), BF),
        ),
        grid_spec=pltpu.PrefetchScalarGridSpec(
            num_scalar_prefetch=2,
            grid=(count,),
            in_specs=[rows_of((1, span, model)), whole(table.shape), whole(down_t.shape)],
            out_specs=[
                rows_of((1, span, model)),
                rows_of((1, span, hidden)),
                rows_of((1, span, hidden)),
            ],
        ),
        compiler_params=params(32),
        cost_estimate=cost(
            2 * count * span * model * hidden, count * span * (4 * model + 6 * hidden)
        ),
        name="stage_one",
    )(start, lengths, tokens, table, down_t)


def fill_padded(padded, left, body, right):
    reach = left.shape[0]
    span = body.shape[0]
    padded[0:reach] = left
    padded[reach : reach + span] = body
    padded[reach + span : 2 * reach + span] = right


def stage_two_kernel(
    place,
    tokens,
    cotangent,
    conv_input,
    left,
    right,
    table,
    conv_t,
    up_t,
    output,
    conv_out_grad,
    sums,
    padded,
):
    span, model = tokens.shape[1], tokens.shape[2]
    hidden = conv_input.shape[2]
    taps = conv_t.shape[0]

    def vec(name, width):
        return table[ROW[name] : ROW[name] + 1, 0:width]

    @pl.when(pl.program_id(0) == 0)
    def _():
        sums[...] = jnp.zeros_like(sums)

    fill_padded(padded, left[0], conv_input[0], right[0])
    total = dot_nt(padded[0:span], conv_t[0])
    for k in range(1, taps):
        total = total + dot_nt(padded[k * DILATION : k * DILATION + span], conv_t[k])
    total = total + vec("conv_bias", hidden)
    unit, inverse = normed(total)
    gain = vec("final_gain", hidden)
    s = unit * gain + vec("final_shift", hidden)
    phi = cumulative(s)
    three = (s * phi).astype(BF)
    slope = phi + s * (PHI_SCALE * jnp.exp(-0.5 * s * s))
    incoming = cotangent[0]
    result = tokens[0].astype(F32) + dot_nt(three, up_t[...]) + vec("up_bias", model)
    output[0] = result.astype(BF)
    q = dot_nn(incoming, up_t[...]) * slope
    grad = back_rows(q, gain, unit, inverse).astype(BF)
    conv_out_grad[0] = grad

    def add(name, values):
        width = values.shape[1]
        sums[ROW[name] : ROW[name] + 1, 0:width] += row_sum(values)

    add("final_gain", q * unit)
    add("final_shift", q)
    add("conv_bias", grad.astype(F32))
    add("up_bias", incoming.astype(F32))
    return three, incoming


def stage_two_body(grid, hb, fold, place, *refs):
    refs, (three_grad, total) = refs[:-2], refs[-2:]
    three, incoming = stage_two_kernel(place, *refs)

    @pl.when(pl.program_id(0) == 0)
    def _():
        total[...] = jnp.zeros_like(total)

    total[...] += dot_tn(incoming, three)

    @pl.when(pl.program_id(0) == pl.num_programs(0) - 1)
    def _():
        write_pieces(grid, fold * hb, place, total, three_grad)


def write_pieces(grid, rows, place, total, pieces):
    lanes = pieces.shape[2]
    for b in range(grid.batch):
        block = total[b * rows : (b + 1) * rows, :].astype(BF)
        for s in range(grid.seq):
            pieces[distance(grid, place, s, b), :, :] = block[:, s * lanes : (s + 1) * lanes]


def stage_two(grid, place, tokens, cotangent, conv_input, left, right, table, conv_t, up_t):
    count, span, model = tokens.shape
    hidden = conv_input.shape[2]
    taps = conv_t.shape[0]
    reach = left.shape[1]
    hb = hidden // grid.batch
    fold = model // hidden
    hl = hidden // grid.seq
    devices = grid.seq * grid.batch
    pieces = (devices, fold * hb, hl)

    def kernel(
        place, tokens, cotangent, conv_input, left, right, table, conv_t, up_t,
        output, conv_out_grad, sums, up_grad, padded, total,
    ):
        stage_two_body(
            grid, hb, fold, place, tokens, cotangent, conv_input, left, right, table, conv_t,
            up_t, output, conv_out_grad, sums, padded, up_grad, total,
        )

    return pl.pallas_call(
        kernel,
        out_shape=(
            sds((count, span, model), BF),
            sds((count, span, hidden), BF),
            sds((TABLE_ROWS, model), F32),
            sds(pieces, BF),
        ),
        grid_spec=pltpu.PrefetchScalarGridSpec(
            num_scalar_prefetch=1,
            grid=(count,),
            in_specs=[
                rows_of((1, span, model)),
                rows_of((1, span, model)),
                rows_of((1, span, hidden)),
                rows_of((1, reach, hidden)),
                rows_of((1, reach, hidden)),
                whole(table.shape),
                whole(conv_t.shape),
                whole(up_t.shape),
            ],
            out_specs=[
                rows_of((1, span, model)),
                rows_of((1, span, hidden)),
                whole((TABLE_ROWS, model)),
                whole(pieces),
            ],
            scratch_shapes=[
                pltpu.VMEM((span + 2 * reach, hidden), BF),
                pltpu.VMEM((model, hidden), F32),
            ],
        ),
        compiler_params=params(56),
        cost_estimate=cost(
            2 * count * span * hidden * (taps * hidden + 3 * model),
            count * span * (6 * model + 4 * hidden),
        ),
        name="stage_two",
    )(place, tokens, cotangent, conv_input, left, right, table, conv_t, up_t)


def stage_three_kernel(
    grid, taps, place, conv_input, left, right, conv_out_grad, pieces, padded, total
):
    group, span, hidden = conv_input.shape
    reach = left.shape[1]

    @pl.when(pl.program_id(0) == 0)
    def _():
        total[...] = jnp.zeros_like(total)

    for g in range(group):
        padded[g, 0:reach] = left[g]
        padded[g, reach : reach + span] = conv_input[g]
        padded[g, reach + span : 2 * reach + span] = right[g]
    flipped = conv_out_grad[...].reshape(group * span, hidden).T
    for k in range(taps):
        window = padded[:, k * DILATION : k * DILATION + span, :].reshape(group * span, hidden)
        total[k] += dot_nn(flipped, window)

    @pl.when(pl.program_id(0) == pl.num_programs(0) - 1)
    def _():
        rows = hidden // grid.batch
        lanes = hidden // grid.seq
        for b in range(grid.batch):
            for k in range(taps):
                block = total[k, b * rows : (b + 1) * rows, :].astype(BF)
                for s in range(grid.seq):
                    pieces[distance(grid, place, s, b), :, k * lanes : (k + 1) * lanes] = block[
                        :, s * lanes : (s + 1) * lanes
                    ]


def stage_three(grid, place, conv_input, left, right, conv_out_grad, taps):
    count, span, hidden = conv_input.shape
    reach = left.shape[1]
    group = 2 if count % 2 == 0 else 1
    pieces = (grid.seq * grid.batch, hidden // grid.batch, taps * (hidden // grid.seq))
    return pl.pallas_call(
        functools.partial(stage_three_kernel, grid, taps),
        out_shape=sds(pieces, BF),
        grid_spec=pltpu.PrefetchScalarGridSpec(
            num_scalar_prefetch=1,
            grid=(count // group,),
            in_specs=[
                rows_of((group, span, hidden)),
                rows_of((group, reach, hidden)),
                rows_of((group, reach, hidden)),
                rows_of((group, span, hidden)),
            ],
            out_specs=whole(pieces),
            scratch_shapes=[
                pltpu.VMEM((group, span + 2 * reach, hidden), BF),
                pltpu.VMEM((taps, hidden, hidden), F32),
            ],
        ),
        compiler_params=params(48),
        cost_estimate=cost(
            2 * count * span * hidden * taps * hidden, count * span * 4 * hidden
        ),
        name="stage_three",
    )(place, conv_input, left, right, conv_out_grad)


def stage_four_kernel(
    grid,
    place,
    start_ref,
    length_ref,
    tokens,
    cotangent,
    hidden_one,
    narrow,
    conv_out_grad,
    left,
    right,
    table,
    sums_in,
    conv_t,
    down_t,
    tokens_grad,
    pieces,
    padded,
    sums,
    total,
):
    span, model = tokens.shape[1], tokens.shape[2]
    hidden = narrow.shape[2]
    taps = conv_t.shape[0]

    def vec(name, width):
        return table[ROW[name] : ROW[name] + 1, 0:width]

    def add(name, values):
        width = values.shape[1]
        sums[ROW[name] : ROW[name] + 1, 0:width] += row_sum(values)

    @pl.when(pl.program_id(0) == 0)
    def _():
        sums[...] = sums_in[...]
        total[...] = jnp.zeros_like(total)

    fill_padded(padded, left[0], conv_out_grad[0], right[0])
    back = None
    for k in range(taps):
        at = (taps - 1 - k) * DILATION
        term = dot_nn(padded[at : at + span], conv_t[k])
        back = term if back is None else back + term
    position = start_ref[0] + lax.broadcasted_iota(jnp.int32, (span, 1), 0)
    valid = (position < length_ref[pl.program_id(0)]).astype(F32)
    back = back * valid
    unit, inverse = normed(narrow[0])
    gain = vec("middle_gain", hidden)
    q = back * gelu_slope(unit * gain + vec("middle_shift", hidden))
    low = back_rows(q, gain, unit, inverse).astype(BF)
    add("middle_gain", q * unit)
    add("middle_shift", q)
    add("down_bias", low.astype(F32))
    total[...] += dot_tn(low, hidden_one[0])
    deep = dot_nn(low, down_t[...])
    unit, inverse = normed(tokens[0].astype(F32))
    gain = vec("first_gain", model)
    q = deep * gelu_slope(unit * gain + vec("first_shift", model))
    add("first_gain", q * unit)
    add("first_shift", q)
    grad = back_rows(q, gain, unit, inverse) + cotangent[0].astype(F32)
    tokens_grad[0] = grad.astype(BF)

    @pl.when(pl.program_id(0) == pl.num_programs(0) - 1)
    def _():
        hb = hidden // grid.batch
        dl = model // grid.seq
        wide = model // grid.batch
        sub = lax.broadcasted_iota(jnp.int32, (16, dl), 0)
        for b in range(grid.batch):
            block = total[b * hb : (b + 1) * hb, :].astype(BF)
            tail = jnp.zeros((16, dl), F32)
            at = 0
            for name in WIDE + NARROW:
                width = wide if name in WIDE else hb
                done = 0
                while done < width:
                    line, col = at // dl, at % dl
                    take = min(width - done, dl - col)
                    first = b * width + done
                    value = sums[ROW[name] : ROW[name] + 1, first : first + take]
                    parts = []
                    if col:
                        parts.append(jnp.zeros((1, col), F32))
                    parts.append(value)
                    if col + take < dl:
                        parts.append(jnp.zeros((1, dl - col - take), F32))
                    spread = jnp.concatenate(parts, axis=1) if len(parts) > 1 else value
                    tail = tail + jnp.where(sub == line, spread, 0.0)
                    at += take
                    done += take
            tail = tail.astype(BF)
            for s in range(grid.seq):
                to = distance(grid, place, s, b)
                pieces[to, 0:hb, :] = block[:, s * dl : (s + 1) * dl]
                pieces[to, hb : hb + 16, :] = tail


def stage_four(
    grid,
    place,
    start,
    lengths,
    tokens,
    cotangent,
    hidden_one,
    narrow,
    conv_out_grad,
    left,
    right,
    table,
    sums,
    conv_t,
    down_t,
):
    count, span, model = tokens.shape
    hidden = narrow.shape[2]
    taps = conv_t.shape[0]
    reach = left.shape[1]
    hb = hidden // grid.batch
    pieces = (grid.seq * grid.batch, hb + 16, model // grid.seq)
    return pl.pallas_call(
        functools.partial(stage_four_kernel, grid),
        out_shape=(sds((count, span, model), BF), sds(pieces, BF)),
        grid_spec=pltpu.PrefetchScalarGridSpec(
            num_scalar_prefetch=3,
            grid=(count,),
            in_specs=[
                rows_of((1, span, model)),
                rows_of((1, span, model)),
                rows_of((1, span, model)),
                rows_of((1, span, hidden)),
                rows_of((1, span, hidden)),
                rows_of((1, reach, hidden)),
                rows_of((1, reach, hidden)),
                whole(table.shape),
                whole(table.shape),
                whole(conv_t.shape),
                whole(down_t.shape),
            ],
            out_specs=[rows_of((1, span, model)), whole(pieces)],
            scratch_shapes=[
                pltpu.VMEM((span + 2 * reach, hidden), BF),
                pltpu.VMEM((TABLE_ROWS, model), F32),
                pltpu.VMEM((hidden, model), F32),
            ],
        ),
        compiler_params=params(56),
        cost_estimate=cost(
            2 * count * span * hidden * (taps * hidden + 2 * model),
            count * span * (8 * model + 6 * hidden),
        ),
        name="stage_four",
    )(
        place, start, lengths, tokens, cotangent, hidden_one, narrow, conv_out_grad, left, right,
        table, sums, conv_t, down_t,
    )


def halos(cells, reach):
    count = lax.axis_size("seq")
    left = lax.ppermute(
        cells[:, cells.shape[1] - reach :], "seq", [(i, i + 1) for i in range(count - 1)]
    )
    right = lax.ppermute(cells[:, :reach], "seq", [(i + 1, i) for i in range(count - 1)])
    return left, right


def body(
    grid,
    tokens,
    lengths,
    first_gain,
    first_shift,
    down_weight,
    down_bias,
    middle_gain,
    middle_shift,
    conv_weight,
    conv_bias,
    final_gain,
    final_shift,
    up_weight,
    up_bias,
    cotangent,
):
    shape = tokens.shape
    span, model = shape[2], shape[3]
    count = shape[0] * shape[1]
    taps = conv_weight.shape[0]
    hb = down_weight.shape[1]
    hidden = hb * grid.batch
    dl, hl = down_weight.shape[0], conv_weight.shape[1]
    fold = model // hidden
    reach = (taps - 1) // 2 * DILATION

    tokens = tokens.reshape(count, span, model)
    cotangent = cotangent.reshape(count, span, model)
    lengths = lengths.reshape(count)
    here = grid.here()
    place = jnp.stack(here).astype(jnp.int32)
    start = (lax.axis_index("seq") * span).astype(jnp.int32).reshape(1)

    vectors = {
        "first_gain": first_gain,
        "first_shift": first_shift,
        "up_bias": up_bias,
        "down_bias": down_bias,
        "middle_gain": middle_gain,
        "middle_shift": middle_shift,
        "conv_bias": conv_bias,
        "final_gain": final_gain,
        "final_shift": final_shift,
    }
    flat = jnp.concatenate([vectors[name] for name in WIDE + NARROW])
    flat = jnp.pad(flat, (0, 16 * dl - flat.shape[0])).reshape(16, dl)
    first_piece = jnp.concatenate([down_weight.T, flat], axis=0)
    second_piece = jnp.concatenate(
        [
            conv_weight.transpose(2, 0, 1).reshape(hb, taps * hl),
            up_weight.T.reshape(fold, hb, hl).transpose(1, 0, 2).reshape(hb, fold * hl),
        ],
        axis=1,
    )
    devices = grid.seq * grid.batch
    gathered = grid.gather(first_piece).reshape((devices,) + first_piece.shape)
    down_t, table = assemble_down(grid, hb, model, gathered, place)
    down_t = down_t.reshape(hidden, model)
    gathered = grid.gather(second_piece).reshape((devices,) + second_piece.shape)
    conv_t, up_t = assemble_rest(grid, hb, hidden, taps, fold, gathered, place)
    conv_t = conv_t.reshape(taps, hidden, hidden)
    up_t = up_t.reshape(model, hidden)

    hidden_one, narrow, conv_input = stage_one(tokens, table, down_t, start, lengths)
    left, right = halos(conv_input, reach)
    block_output, conv_out_grad, sums, up_pieces = stage_two(
        grid, place, tokens, cotangent, conv_input, left, right, table, conv_t, up_t
    )
    grad_left, grad_right = halos(conv_out_grad, reach)
    conv_pieces = stage_three(grid, place, conv_input, left, right, conv_out_grad, taps)
    tokens_grad, down_pieces = stage_four(
        grid, place, start, lengths, tokens, cotangent, hidden_one, narrow, conv_out_grad,
        grad_left, grad_right, table, sums, conv_t, down_t,
    )

    spread = (2, grid.side, grid.side, grid.depth)
    up_piece = grid.scatter(up_pieces.reshape(spread + up_pieces.shape[1:]))
    conv_piece = grid.scatter(conv_pieces.reshape(spread + conv_pieces.shape[1:]))
    down_piece = grid.scatter(down_pieces.reshape(spread + down_pieces.shape[1:]))

    up_grad = up_piece.T
    conv_grad = conv_piece.reshape(hb, taps, hl).transpose(1, 2, 0)
    down_grad = down_piece[:hb].T
    tail = down_piece[hb:].reshape(-1)
    grads = {}
    at = 0
    for name in WIDE + NARROW:
        width = vectors[name].shape[0]
        grads[name] = tail[at : at + width]
        at += width
    return (
        block_output.reshape(shape),
        tokens_grad.reshape(shape),
        grads["first_gain"],
        grads["first_shift"],
        down_grad,
        grads["down_bias"],
        grads["middle_gain"],
        grads["middle_shift"],
        conv_grad,
        grads["conv_bias"],
        grads["final_gain"],
        grads["final_shift"],
        up_grad,
        grads["up_bias"],
    )


def solution(mesh):
    grid = Grid(mesh.shape["seq"], mesh.shape["batch"])
    return jax.shard_map(
        functools.partial(body, grid),
        mesh=mesh,
        in_specs=(
            P(None, "batch", "seq", None),
            P(None, "batch"),
            P("batch"),
            P("batch"),
            P("seq", "batch"),
            P("batch"),
            P("batch"),
            P("batch"),
            P(None, "seq", "batch"),
            P("batch"),
            P("batch"),
            P("batch"),
            P("seq", "batch"),
            P("batch"),
            P(None, "batch", "seq", None),
        ),
        out_specs=(
            P(None, "batch", "seq", None),
            P(None, "batch", "seq", None),
            P("batch"),
            P("batch"),
            P("seq", "batch"),
            P("batch"),
            P("batch"),
            P("batch"),
            P(None, "seq", "batch"),
            P("batch"),
            P("batch"),
            P("batch"),
            P("seq", "batch"),
            P("batch"),
        ),
        check_vma=False,
    )
```

time: 581 us -> 327 us (0.56)
  matrix products: 135 us -> 0 us
  blocking collectives: 130 us -> 0 us
  Pallas kernels: 0 us -> 120 us
  other arithmetic: 95.4 us -> 19.9 us
  starting transfers between devices: 25.2 us -> 65.4 us
  local copies, waits for them, and re-layouts: 55.5 us -> 26.2 us
  waiting for transfers between devices: 115 us -> 93.7 us
  between operations: 18.2 us -> 1.4 us
    dot_general x42 -> x0, matrix products: 135 us -> none  [the longest x14 73.3 us: contract_cols(): lax.dot_general(left_side, right_side, (((1,), (1,)), ((), ())), preferre...]
    pallas_call x0 -> x6, Pallas kernels: none -> 120 us  [the longest x1 40.3 us: stage_four(): pl.pallas_call(functools.partial(stage_four_kernel, grid), out_shape=(sds...]
    ppermute x8 -> x44, waiting for transfers between devices: 14.6 us -> 93.7 us  [the longest x40 93.7 us: send(): return lax.ppermute(value, ('seq', 'batch'), pairs)]
    unnamed x12 -> x0, waiting for transfers between devices: 65.3 us -> none
    all_gather x3 -> x0, blocking collectives: 59.3 us -> none  [the longest x1 27 us: fetch(): lax.all_gather(conv_weight, 'batch', axis=2, tiled=True)]
    unnamed x2 -> x0, blocking collectives: 59.2 us -> none
    ppermute x8 -> x44, starting transfers between devices: 24.5 us -> 65.4 us  [the longest x40 54.6 us: send(): return lax.ppermute(value, ('seq', 'batch'), pairs)]
    convert_element_type x14 -> x12, other arithmetic: 46.5 us -> 6.29 us  [add(): return total.astype(kind)]
  transfers between devices with their start and end apart: 17 -> 44, of which waited for: 11 -> 23; matrix products, arithmetic and copies ran while one was open for 34% -> 8% of each run, Pallas kernels for 0% -> 25%
where the time goes in v1:
time: 327 us
  Pallas kernels  120 us (37%)
  waiting for transfers between devices  93.7 us (29%)
  starting transfers between devices  65.4 us (20%)
  local copies, waits for them, and re-layouts  26.2 us (8%)
  other arithmetic  19.9 us (6%)
    ppermute x40, waiting for transfers between devices, send(): return lax.ppermute(value, ('seq', 'batch'), pairs)  93.7 us
    ppermute x40, starting transfers between devices, send(): return lax.ppermute(value, ('seq', 'batch'), pairs)  54.6 us
    pallas_call x1, Pallas kernels, stage_four(): pl.pallas_call(functools.partial(stage_four_kernel, grid), out_shape=(sds...  40.3 us
    pallas_call x1, Pallas kernels, stage_two(): pl.pallas_call(kernel, out_shape=(sds((count, span, model), BF), sds((cou...  39.7 us
    pallas_call x1, Pallas kernels, stage_three(): pl.pallas_call(functools.partial(stage_three_kernel, grid, taps), out_sha...  15.7 us
    pallas_call x1, Pallas kernels, stage_one(): pl.pallas_call(stage_one_kernel, out_shape=(sds((count, span, model), BF)...  12.4 us
    another operation x4, other arithmetic, gather(): return jnp.stack([mine, other])  12 us
    pallas_call x1, Pallas kernels, assemble_rest(): pl.pallas_call(functools.partial(assemble_rest_kernel, grid, hb, hl, taps...  10.9 us
  transfers between devices with their start and end apart: 44, of which 23 were waited for; matrix products, arithmetic and copies ran while one was open for 8% of the time, Pallas kernels for 25%

profile of v1, /device:TPU:0, one launch (start us, length us, event | category | flops | bytes accessed | tf_op | source)
XLA Modules:
  0.0 326.7 jit_solution(1492793144005641862)
XLA Ops:
  3.0 4.1 %collective-permute-start.13 = (bf16[80,1120]{1,0:T(8,128)(2,1)S(1)}, bf16[80,1120]{1,0:T(8,128)(2,1)S(1)}, u32[]{:S(2)}, u32[]{:S(2)}) collective-permute-start(bf16[80,1120]{1,0:T(8,128)(2,1)S(1)} %pad_maximum_fusion.8), channel_id=1, source_target_pairs={{0,4},{1,5},{2,6},{3,7},{4,0},{5,1},{6,2},{7,3},{8,12},{9,13},{10,... | collective-permute-start | bytes 537608 | tf_op jit(solution)/shard_map/ppermute | solution.py:42
  9.2 8.2 %collective-permute-done.13 = bf16[80,1120]{1,0:T(8,128)(2,1)S(1)} collective-permute-done((bf16[80,1120]{1,0:T(8,128)(2,1)S(1)}, bf16[80,1120]{1,0:T(8,128)(2,1)S(1)}, u32[]{:S(2)}, u32[]{:S(2)}) %collective-permute-start.13) | collective-permute-done | bytes 179232 | tf_op jit(solution)/shard_map/ppermute | solution.py:42
  22.5 3.1 collective-permute-done.15
  27.3 5.2 %collective-permute-done.11 = bf16[2,80,1120]{2,1,0:T(8,128)(2,1)S(1)} collective-permute-done((bf16[2,80,1120]{2,1,0:T(8,128)(2,1)S(1)}, bf16[2,80,1120]{2,1,0:T(8,128)(2,1)S(1)}, u32[]{:S(2)}, u32[]{:S(2)}) %collective-permute-start.11) | collective-permute-done | bytes 358432 | tf_op jit(solution)/shard_map/ppermute | solution.py:42
  34.2 12.0 %collective-permute-done.16 = bf16[2,2,80,1120]{3,2,1,0:T(8,128)(2,1)S(1)} collective-permute-done((bf16[2,2,80,1120]{3,2,1,0:T(8,128)(2,1)S(1)}, bf16[2,2,80,1120]{3,2,1,0:T(8,128)(2,1)S(1)}, u32[]{:S(2)}, u32[]{:S(2)}) %collective-permute-start.16) | collective-permute-done | bytes 716832 | tf_op jit(solution)/shard_map/ppermute | solution.py:42
  50.3 7.7 %collective-permute-start.3 = (bf16[96,320]{1,0:T(8,128)(2,1)S(1)}, bf16[96,320]{1,0:T(8,128)(2,1)S(1)}, u32[]{:S(2)}, u32[]{:S(2)}) collective-permute-start(bf16[96,320]{1,0:T(8,128)(2,1)S(1)} %get-tuple-element.83), channel_id=1, source_target_pairs={{0,4},{1,5},{2,6},{3,7},{4,0},{5,1},{6,2},{7,3},{8,12},{9,13},{10,... | collective-permute-start | bytes 184328 | tf_op jit(solution)/shard_map/ppermute | solution.py:42
  74.3 4.8 %collective-permute-done.6 = bf16[2,2,96,320]{3,2,1,0:T(8,128)(2,1)S(1)} collective-permute-done((bf16[2,2,96,320]{3,2,1,0:T(8,128)(2,1)S(1)}, bf16[2,2,96,320]{3,2,1,0:T(8,128)(2,1)S(1)}, u32[]{:S(2)}, u32[]{:S(2)}) %collective-permute-start.6) | collective-permute-done | bytes 245792 | tf_op jit(solution)/shard_map/ppermute | solution.py:42
  88.1 12.4 %stage_one.1 = (bf16[8,256,1280]{2,1,0:T(8,128)(2,1)S(1)}, f32[8,256,640]{2,1,0:T(8,128)S(1)}, bf16[8,256,640]{2,1,0:T(8,128)(2,1)S(1)}) custom-call(s32[1]{0:T(128)} %bitcast.6.start_ref, s32[8]{0:T(128)S(1)} %reshape.133.length_ref, bf16[8,256,1280]{2,1,0:T(8,128)(2,1)S(1)} %bitcast.210, f32[16,1280]{1,0:T(8,128)S(1)} %get-tuple-element.27.table, ...), custom_call_target="tpu_custom_call" | custom-call | flops 3355443200 | bytes 18350080 | tf_op jit(solution)/shard_map/stage_one/pallas_call | solution.py:268
  100.6 3.3 %collective-permute-start.8 = (bf16[8,32,640]{2,1,0:T(8,128)(2,1)S(1)}, bf16[8,32,640]{2,1,0:T(8,128)(2,1)S(1)}, u32[]{:S(2)}, u32[]{:S(2)}) collective-permute-start(bf16[8,32,640]{2,1,0:T(8,128)(2,1)S(1)} %get-tuple-element.49), channel_id=1, source_target_pairs={{0,8},{8,16},{16,24},{1,9},{9,17},{17,25},{2,10},{10,18},{18,26},{... | collective-permute-start | bytes 983048 | tf_op jit(solution)/shard_map/ppermute | solution.py:665
  105.4 5.9 %pad_maximum_fusion = bf16[2,2,2,4,80,1120]{5,4,3,2,1,0:T(8,128)(2,1)} fusion(bf16[1,2,2,4,80,1120]{5,4,3,2,1,0:T(8,128)(2,1)} %bitcast.43, bf16[1,2,2,4,80,1120]{5,4,3,2,1,0:T(8,128)(2,1)} %get-tuple-element.42), kind=kLoop, calls=%fused_computation | loop fusion | flops 2867200 | bytes 11468800 | tf_op jit(solution)/shard_map/stack | solution.py:66
  111.4 10.9 %assemble_rest.1 = (bf16[5,8,80,640]{3,2,1,0:T(8,128)(2,1)S(1)}, bf16[8,2,80,640]{3,2,1,0:T(8,128)(2,1)S(1)}) custom-call(s32[4]{0:T(128)S(1)} %pad_add_fusion.place, bf16[32,80,1120]{2,1,0:T(8,128)(2,1)} %bitcast.216), custom_call_target="tpu_custom_call" | custom-call | bytes 11468800 | tf_op jit(solution)/shard_map/assemble_rest/pallas_call | solution.py:222
  126.2 39.7 %stage_two.1 = (bf16[8,256,1280]{2,1,0:T(8,128)(2,1)}, bf16[8,256,640]{2,1,0:T(8,128)(2,1)}, f32[16,1280]{1,0:T(8,128)}, bf16[32,160,160]{2,1,0:T(8,128)(2,1)}) custom-call(s32[4]{0:T(128)} %copy-done.3, bf16[8,256,1280]{2,1,0:T(8,128)(2,1)} %bitcast.206, bf16[8,256,1280]{2,1,0:T(8,128)(2,1)} %bitcast.242, bf16[8,256,640]{2,1,0:T(8,128)(2,1)} %copy-done, ...), custom_call_target="tpu_custom_call" | custom-call | flops 18454937600 | bytes 20971520 | tf_op jit(solution)/shard_map/stage_two/pallas_call | solution.py:399
  174.9 4.6 %collective-permute-start.18 = (bf16[8,32,640]{2,1,0:T(8,128)(2,1)S(1)}, bf16[8,32,640]{2,1,0:T(8,128)(2,1)S(1)}, u32[]{:S(2)}, u32[]{:S(2)}) collective-permute-start(bf16[8,32,640]{2,1,0:T(8,128)(2,1)S(1)} %get-tuple-element.47), channel_id=1, source_target_pairs={{0,8},{8,16},{16,24},{1,9},{9,17},{17,25},{2,10},{10,18},{18,26},{... | collective-permute-start | bytes 983048 | tf_op jit(solution)/shard_map/ppermute | solution.py:665
  182.8 15.7 %stage_three.1 = bf16[32,80,800]{2,1,0:T(8,128)(2,1)} custom-call(s32[4]{0:T(128)S(1)} %copy-done.4, bf16[8,256,640]{2,1,0:T(8,128)(2,1)S(1)} %copy-done.1, bf16[8,32,640]{2,1,0:T(8,128)(2,1)S(1)} %copy-done.9, bf16[8,32,640]{2,1,0:T(8,128)(2,1)S(1)} %copy-done.11, bf16[8,256,640]{2,1,0:T(8,128)(2,1)S(1)} %copy-done.2), custom_call_target="tpu_custom_call" | custom-call | flops 8388608000 | bytes 5242880 | tf_op jit(solution)/shard_map/stage_three/pallas_call | solution.py:477
  202.3 40.3 %stage_four.1 = (bf16[8,256,1280]{2,1,0:T(8,128)(2,1)}, bf16[32,96,320]{2,1,0:T(8,128)(2,1)}) custom-call(s32[4]{0:T(128)} %copy-done.3, s32[1]{0:T(128)} %bitcast.6.start_ref, s32[8]{0:T(128)} %copy-done.13, bf16[8,256,1280]{2,1,0:T(8,128)(2,1)} %bitcast.207, bf16[8,256,1280]{2,1,0:T(8,128)(2,1)} %bitcast.243, bf16[8,256,1280]{2,1,0:T(8,128)(2,1)} %copy-done.14, ...), custom_call_target="tpu_custom_call" | custom-call | flops 15099494400 | bytes 28835840 | tf_op jit(solution)/shard_map/stage_four/pallas_call | solution.py:625
  244.5 4.6 %collective-permute-start.37 = (bf16[2,2,160,160]{2,3,1,0:T(8,128)(2,1)S(1)}, bf16[2,2,160,160]{2,3,1,0:T(8,128)(2,1)S(1)}, u32[]{:S(2)}, u32[]{:S(2)}) collective-permute-start(bf16[2,2,160,160]{2,3,1,0:T(8,128)(2,1)S(1)} %slice_bitcast_fusion.6), channel_id=1, source_target_pairs={{0,16},{1,17},{2,18},{3,19},{4,20},{5,21},{6,22},{7,23},{8,24},{9,... | collective-permute-start | bytes 614408 | tf_op jit(solution)/shard_map/ppermute | solution.py:42
  249.6 7.8 %collective-permute-done.37 = bf16[2,2,160,160]{2,3,1,0:T(8,128)(2,1)S(1)} collective-permute-done((bf16[2,2,160,160]{2,3,1,0:T(8,128)(2,1)S(1)}, bf16[2,2,160,160]{2,3,1,0:T(8,128)(2,1)S(1)}, u32[]{:S(2)}, u32[]{:S(2)}) %collective-permute-start.37) | collective-permute-done | bytes 204832 | tf_op jit(solution)/shard_map/ppermute | solution.py:42
  259.9 4.8 %collective-permute-done.38 = bf16[2,160,160]{1,2,0:T(8,128)(2,1)S(1)} collective-permute-done((bf16[2,160,160]{1,2,0:T(8,128)(2,1)S(1)}, bf16[2,160,160]{1,2,0:T(8,128)(2,1)S(1)}, u32[]{:S(2)}, u32[]{:S(2)}) %collective-permute-start.38) | collective-permute-done | bytes 102432 | tf_op jit(solution)/shard_map/ppermute | solution.py:42
  268.5 4.1 %collective-permute-done.21 = bf16[2,2,96,320]{3,2,1,0:T(8,128)(2,1)S(1)} collective-permute-done((bf16[2,2,96,320]{3,2,1,0:T(8,128)(2,1)S(1)}, bf16[2,2,96,320]{3,2,1,0:T(8,128)(2,1)S(1)}, u32[]{:S(2)}, u32[]{:S(2)}) %collective-permute-start.21) | collective-permute-done | bytes 245792 | tf_op jit(solution)/shard_map/ppermute | solution.py:42
  275.6 4.2 %collective-permute-done.22 = bf16[2,96,320]{2,1,0:T(8,128)(2,1)S(1)} collective-permute-done((bf16[2,96,320]{2,1,0:T(8,128)(2,1)S(1)}, bf16[2,96,320]{2,1,0:T(8,128)(2,1)S(1)}, u32[]{:S(2)}, u32[]{:S(2)}) %collective-permute-start.22) | collective-permute-done | bytes 122912 | tf_op jit(solution)/shard_map/ppermute | solution.py:42
  280.9 4.0 %collective-permute-done.25 = bf16[2,96,320]{2,1,0:T(8,128)(2,1)S(1)} collective-permute-done((bf16[2,96,320]{2,1,0:T(8,128)(2,1)S(1)}, bf16[2,96,320]{2,1,0:T(8,128)(2,1)S(1)}, u32[]{:S(2)}, u32[]{:S(2)}) %collective-permute-start.25) | collective-permute-done | bytes 122912 | tf_op jit(solution)/shard_map/ppermute | solution.py:42
  298.2 4.1 %collective-permute-done.29 = bf16[2,2,80,800]{3,2,1,0:T(8,128)(2,1)S(1)} collective-permute-done((bf16[2,2,80,800]{3,2,1,0:T(8,128)(2,1)}, bf16[2,2,80,800]{3,2,1,0:T(8,128)(2,1)S(1)}, u32[]{:S(2)}, u32[]{:S(2)}) %collective-permute-start.29) | collective-permute-done | bytes 512032 | tf_op jit(solution)/shard_map/ppermute | solution.py:42
  308.9 4.5 %collective-permute-done.30 = bf16[2,80,800]{2,1,0:T(8,128)(2,1)S(1)} collective-permute-done((bf16[2,80,800]{2,1,0:T(8,128)(2,1)S(1)}, bf16[2,80,800]{2,1,0:T(8,128)(2,1)S(1)}, u32[]{:S(2)}, u32[]{:S(2)}) %collective-permute-start.30) | collective-permute-done | bytes 256032 | tf_op jit(solution)/shard_map/ppermute | solution.py:42
  320.0 5.7 %collective-permute-done.34 = bf16[80,800]{1,0:T(8,128)(2,1)S(1)} collective-permute-done((bf16[80,800]{1,0:T(8,128)(2,1)S(1)}, bf16[80,800]{1,0:T(8,128)(2,1)S(1)}, u32[]{:S(2)}, u32[]{:S(2)}) %collective-permute-start.34) | collective-permute-done | bytes 128032 | tf_op jit(solution)/shard_map/ppermute | solution.py:42
  (208 shorter events, 103.4 us)
Async XLA Ops:
  3.0 14.3 %collective-permute-start.13 = (bf16[80,1120]{1,0:T(8,128)(2,1)S(1)}, bf16[80,1120]{1,0:T(8,128)(2,1)S(1)}, u32[]{:S(2)}, u32[]{:S(2)}) collective-permute-start(bf16[80,1120]{1,0:T(8,128)(2,1)S(1)} %pad_maximum_fusion.8), channel_id=1, source_target_pairs={{0,4},{1,5},{2,6},{3,7},{4,0},{5,1},{6,2},{7,3},{8,12},{9,13},{10,... | collective-permute-start | bytes 537608 | tf_op jit(solution)/shard_map/ppermute | solution.py:42
  7.1 10.2 %collective-permute-start.14 = (bf16[80,1120]{1,0:T(8,128)(2,1)S(1)}, bf16[80,1120]{1,0:T(8,128)(2,1)S(1)}, u32[]{:S(2)}, u32[]{:S(2)}) collective-permute-start(bf16[80,1120]{1,0:T(8,128)(2,1)S(1)} %pad_maximum_fusion.8), channel_id=1, source_target_pairs={{0,6},{1,7},{2,0},{3,1},{4,2},{5,3},{6,4},{7,5},{8,14},{9,15},{10,... | collective-permute-start | bytes 537608 | tf_op jit(solution)/shard_map/ppermute | solution.py:42
  8.5 12.4 %collective-permute-start.10 = (bf16[80,1120]{1,0:T(8,128)(2,1)S(1)}, bf16[80,1120]{1,0:T(8,128)(2,1)S(1)}, u32[]{:S(2)}, u32[]{:S(2)}) collective-permute-start(bf16[80,1120]{1,0:T(8,128)(2,1)S(1)} %pad_maximum_fusion.8), channel_id=1, source_target_pairs={{0,2},{1,3},{2,4},{3,5},{4,6},{5,7},{6,0},{7,1},{8,10},{9,11},{10,... | collective-permute-start | bytes 537608 | tf_op jit(solution)/shard_map/ppermute | solution.py:42
  21.0 11.6 %collective-permute-start.11 = (bf16[2,80,1120]{2,1,0:T(8,128)(2,1)S(1)}, bf16[2,80,1120]{2,1,0:T(8,128)(2,1)S(1)}, u32[]{:S(2)}, u32[]{:S(2)}) collective-permute-start(bf16[2,80,1120]{2,1,0:T(8,128)(2,1)S(1)} %get-tuple-element.65), channel_id=1, source_target_pairs={{0,8},{1,9},{2,10},{3,11},{4,12},{5,13},{6,14},{7,15},{8,0},{9,1},... | collective-permute-start | bytes 1075208 | tf_op jit(solution)/shard_map/ppermute | solution.py:42
  25.7 20.5 %collective-permute-start.16 = (bf16[2,2,80,1120]{3,2,1,0:T(8,128)(2,1)S(1)}, bf16[2,2,80,1120]{3,2,1,0:T(8,128)(2,1)S(1)}, u32[]{:S(2)}, u32[]{:S(2)}) collective-permute-start(bf16[2,2,80,1120]{3,2,1,0:T(8,128)(2,1)S(1)} %get-tuple-element.63), channel_id=1, source_target_pairs={{0,8},{1,9},{2,10},{3,11},{4,12},{5,13},{6,14},{7,15},{8,0},{9,1},... | collective-permute-start | bytes 2150408 | tf_op jit(solution)/shard_map/ppermute | solution.py:42
  32.7 14.4 %collective-permute-start.12 = (bf16[2,2,80,1120]{3,2,1,0:T(8,128)(2,1)S(1)}, bf16[2,2,80,1120]{3,2,1,0:T(8,128)(2,1)S(1)}, u32[]{:S(2)}, u32[]{:S(2)}) collective-permute-start(bf16[2,2,80,1120]{3,2,1,0:T(8,128)(2,1)S(1)} %get-tuple-element.61), channel_id=1, source_target_pairs={{0,16},{1,17},{2,18},{3,19},{4,20},{5,21},{6,22},{7,23},{8,24},{9,... | collective-permute-start | bytes 2150408 | tf_op jit(solution)/shard_map/ppermute | solution.py:42
  50.0 55.5 %collective-permute-start.17 = (bf16[2,2,4,80,1120]{4,3,2,1,0:T(8,128)(2,1)}, bf16[2,2,4,80,1120]{4,3,2,1,0:T(8,128)(2,1)}, u32[]{:S(2)}, u32[]{:S(2)}) collective-permute-start(bf16[2,2,4,80,1120]{4,3,2,1,0:T(8,128)(2,1)} %get-tuple-element.43), channel_id=1, source_target_pairs={{0,1},{1,0},{2,3},{3,2},{4,5},{5,4},{6,7},{7,6},{8,9},{9,8},{10,11... | collective-permute-start | bytes 8601608 | tf_op jit(solution)/shard_map/ppermute | solution.py:42
  50.3 11.6 %collective-permute-start.3 = (bf16[96,320]{1,0:T(8,128)(2,1)S(1)}, bf16[96,320]{1,0:T(8,128)(2,1)S(1)}, u32[]{:S(2)}, u32[]{:S(2)}) collective-permute-start(bf16[96,320]{1,0:T(8,128)(2,1)S(1)} %get-tuple-element.83), channel_id=1, source_target_pairs={{0,4},{1,5},{2,6},{3,7},{4,0},{5,1},{6,2},{7,3},{8,12},{9,13},{10,... | collective-permute-start | bytes 184328 | tf_op jit(solution)/shard_map/ppermute | solution.py:42
  100.6 24.7 %collective-permute-start.8 = (bf16[8,32,640]{2,1,0:T(8,128)(2,1)S(1)}, bf16[8,32,640]{2,1,0:T(8,128)(2,1)S(1)}, u32[]{:S(2)}, u32[]{:S(2)}) collective-permute-start(bf16[8,32,640]{2,1,0:T(8,128)(2,1)S(1)} %get-tuple-element.49), channel_id=1, source_target_pairs={{0,8},{8,16},{16,24},{1,9},{9,17},{17,25},{2,10},{10,18},{18,26},{... | collective-permute-start | bytes 983048 | tf_op jit(solution)/shard_map/ppermute | solution.py:665
  103.9 21.4 %collective-permute-start.9 = (bf16[8,32,640]{2,1,0:T(8,128)(2,1)S(1)}, bf16[8,32,640]{2,1,0:T(8,128)(2,1)S(1)}, u32[]{:S(2)}, u32[]{:S(2)}) collective-permute-start(bf16[8,32,640]{2,1,0:T(8,128)(2,1)S(1)} %get-tuple-element.48), channel_id=1, source_target_pairs={{8,0},{16,8},{24,16},{9,1},{17,9},{25,17},{10,2},{18,10},{26,18},{... | collective-permute-start | bytes 983048 | tf_op jit(solution)/shard_map/ppermute | solution.py:668
  170.6 72.0 %collective-permute-start.36 = (bf16[2,2,4,160,160]{3,4,2,1,0:T(8,128)(2,1)}, bf16[2,2,4,160,160]{3,4,2,1,0:T(8,128)(2,1)}, u32[]{:S(2)}, u32[]{:S(2)}) collective-permute-start(bf16[2,2,4,160,160]{3,4,2,1,0:T(8,128)(2,1)} %copy.37), channel_id=1, source_target_pairs={{0,1},{1,0},{2,3},{3,2},{4,5},{5,4},{6,7},{7,6},{8,9},{9,8},{10,11... | collective-permute-start | bytes 2457608 | tf_op jit(solution)/shard_map/ppermute | solution.py:42
  174.9 26.5 %collective-permute-start.18 = (bf16[8,32,640]{2,1,0:T(8,128)(2,1)S(1)}, bf16[8,32,640]{2,1,0:T(8,128)(2,1)S(1)}, u32[]{:S(2)}, u32[]{:S(2)}) collective-permute-start(bf16[8,32,640]{2,1,0:T(8,128)(2,1)S(1)} %get-tuple-element.47), channel_id=1, source_target_pairs={{0,8},{8,16},{16,24},{1,9},{9,17},{17,25},{2,10},{10,18},{18,26},{... | collective-permute-start | bytes 983048 | tf_op jit(solution)/shard_map/ppermute | solution.py:665
  179.5 22.0 %collective-permute-start.19 = (bf16[8,32,640]{2,1,0:T(8,128)(2,1)S(1)}, bf16[8,32,640]{2,1,0:T(8,128)(2,1)S(1)}, u32[]{:S(2)}, u32[]{:S(2)}) collective-permute-start(bf16[8,32,640]{2,1,0:T(8,128)(2,1)S(1)} %get-tuple-element.46), channel_id=1, source_target_pairs={{8,0},{16,8},{24,16},{9,1},{17,9},{25,17},{10,2},{18,10},{26,18},{... | collective-permute-start | bytes 983048 | tf_op jit(solution)/shard_map/ppermute | solution.py:668
  201.1 86.0 %collective-permute-start.28 = (bf16[2,2,4,80,800]{4,3,2,1,0:T(8,128)(2,1)S(1)}, bf16[2,2,4,80,800]{4,3,2,1,0:T(8,128)(2,1)}, u32[]{:S(2)}, u32[]{:S(2)}) collective-permute-start(bf16[2,2,4,80,800]{4,3,2,1,0:T(8,128)(2,1)S(1)} %bitcast.221), channel_id=1, source_target_pairs={{0,1},{1,0},{2,3},{3,2},{4,5},{5,4},{6,7},{7,6},{8,9},{9,8},{10,11... | collective-permute-start | bytes 6144008 | tf_op jit(solution)/shard_map/ppermute | solution.py:42
  244.5 13.0 %collective-permute-start.37 = (bf16[2,2,160,160]{2,3,1,0:T(8,128)(2,1)S(1)}, bf16[2,2,160,160]{2,3,1,0:T(8,128)(2,1)S(1)}, u32[]{:S(2)}, u32[]{:S(2)}) collective-permute-start(bf16[2,2,160,160]{2,3,1,0:T(8,128)(2,1)S(1)} %slice_bitcast_fusion.6), channel_id=1, source_target_pairs={{0,16},{1,17},{2,18},{3,19},{4,20},{5,21},{6,22},{7,23},{8,24},{9,... | collective-permute-start | bytes 614408 | tf_op jit(solution)/shard_map/ppermute | solution.py:42
  249.1 9.8 %collective-permute-start.40 = (bf16[2,2,160,160]{2,3,1,0:T(8,128)(2,1)S(1)}, bf16[2,2,160,160]{2,3,1,0:T(8,128)(2,1)S(1)}, u32[]{:S(2)}, u32[]{:S(2)}) collective-permute-start(bf16[2,2,160,160]{2,3,1,0:T(8,128)(2,1)S(1)} %slice_bitcast_fusion.4), channel_id=1, source_target_pairs={{0,8},{1,9},{2,10},{3,11},{4,12},{5,13},{6,14},{7,15},{8,0},{9,1},... | collective-permute-start | bytes 614408 | tf_op jit(solution)/shard_map/ppermute | solution.py:42
  249.4 15.5 %collective-permute-start.20 = (bf16[2,2,4,96,320]{4,3,2,1,0:T(8,128)(2,1)S(1)}, bf16[2,2,4,96,320]{4,3,2,1,0:T(8,128)(2,1)S(1)}, u32[]{:S(2)}, u32[]{:S(2)}) collective-permute-start(bf16[2,2,4,96,320]{4,3,2,1,0:T(8,128)(2,1)S(1)} %bitcast.222), channel_id=1, source_target_pairs={{0,1},{1,0},{2,3},{3,2},{4,5},{5,4},{6,7},{7,6},{8,9},{9,8},{10,11... | collective-permute-start | bytes 2949128 | tf_op jit(solution)/shard_map/ppermute | solution.py:42
  264.8 26.5 %collective-permute-start.39 = (bf16[160,160]{0,1:T(8,128)(2,1)S(1)}, bf16[160,160]{0,1:T(8,128)(2,1)S(1)}, u32[]{:S(2)}, u32[]{:S(2)}) collective-permute-start(bf16[160,160]{0,1:T(8,128)(2,1)S(1)} %slice_bitcast_fusion.31), channel_id=1, source_target_pairs={{0,6},{1,7},{2,0},{3,1},{4,2},{5,3},{6,4},{7,5},{8,14},{9,15},{10,... | collective-permute-start | bytes 153608 | tf_op jit(solution)/shard_map/ppermute | solution.py:42
  266.3 25.6 %collective-permute-start.42 = (bf16[160,160]{0,1:T(8,128)(2,1)S(1)}, bf16[160,160]{0,1:T(8,128)(2,1)S(1)}, u32[]{:S(2)}, u32[]{:S(2)}) collective-permute-start(bf16[160,160]{0,1:T(8,128)(2,1)S(1)} %get-tuple-element.74), channel_id=1, source_target_pairs={{0,4},{1,5},{2,6},{3,7},{4,0},{5,1},{6,2},{7,3},{8,12},{9,13},{10,... | collective-permute-start | bytes 153608 | tf_op jit(solution)/shard_map/ppermute | solution.py:42
  272.7 20.4 %collective-permute-start.43 = (bf16[160,160]{0,1:T(8,128)(2,1)S(1)}, bf16[160,160]{0,1:T(8,128)(2,1)S(1)}, u32[]{:S(2)}, u32[]{:S(2)}) collective-permute-start(bf16[160,160]{0,1:T(8,128)(2,1)S(1)} %get-tuple-element.75), channel_id=1, source_target_pairs={{0,2},{1,3},{2,4},{3,5},{4,6},{5,7},{6,0},{7,1},{8,10},{9,11},{10,... | collective-permute-start | bytes 153608 | tf_op jit(solution)/shard_map/ppermute | solution.py:42
  284.9 9.7 %collective-permute-start.23 = (bf16[96,320]{1,0:T(8,128)(2,1)S(1)}, bf16[96,320]{1,0:T(8,128)(2,1)S(1)}, u32[]{:S(2)}, u32[]{:S(2)}) collective-permute-start(bf16[96,320]{1,0:T(8,128)(2,1)S(1)} %slice_bitcast_fusion.35), channel_id=1, source_target_pairs={{0,6},{1,7},{2,0},{3,1},{4,2},{5,3},{6,4},{7,5},{8,14},{9,15},{10,... | collective-permute-start | bytes 184328 | tf_op jit(solution)/shard_map/ppermute | solution.py:42
  291.9 10.4 %collective-permute-start.29 = (bf16[2,2,80,800]{3,2,1,0:T(8,128)(2,1)}, bf16[2,2,80,800]{3,2,1,0:T(8,128)(2,1)S(1)}, u32[]{:S(2)}, u32[]{:S(2)}) collective-permute-start(bf16[2,2,80,800]{3,2,1,0:T(8,128)(2,1)} %slice_bitcast_fusion.2), channel_id=1, source_target_pairs={{0,16},{1,17},{2,18},{3,19},{4,20},{5,21},{6,22},{7,23},{8,24},{9,... | collective-permute-start | bytes 1536008 | tf_op jit(solution)/shard_map/ppermute | solution.py:42
  293.0 12.4 %collective-permute-start.32 = (bf16[2,2,80,800]{3,2,1,0:T(8,128)(2,1)}, bf16[2,2,80,800]{3,2,1,0:T(8,128)(2,1)}, u32[]{:S(2)}, u32[]{:S(2)}) collective-permute-start(bf16[2,2,80,800]{3,2,1,0:T(8,128)(2,1)} %slice_bitcast_fusion), channel_id=1, source_target_pairs={{0,8},{1,9},{2,10},{3,11},{4,12},{5,13},{6,14},{7,15},{8,0},{9,1},... | collective-permute-start | bytes 1536008 | tf_op jit(solution)/shard_map/ppermute | solution.py:42
  316.5 9.1 %collective-permute-start.34 = (bf16[80,800]{1,0:T(8,128)(2,1)S(1)}, bf16[80,800]{1,0:T(8,128)(2,1)S(1)}, u32[]{:S(2)}, u32[]{:S(2)}) collective-permute-start(bf16[80,800]{1,0:T(8,128)(2,1)S(1)} %get-tuple-element.72), channel_id=1, source_target_pairs={{0,4},{1,5},{2,6},{3,7},{4,0},{5,1},{6,2},{7,3},{8,12},{9,13},{10,... | collective-permute-start | bytes 384008 | tf_op jit(solution)/shard_map/ppermute | solution.py:42
  (53 other events, 375.9 us)

commit v2 on v1

v2 whole, which is shorter than its diff:
```python
import functools
import math

import jax
import jax.numpy as jnp
from jax import lax
from jax.experimental import pallas as pl
from jax.experimental.pallas import tpu as pltpu
from jax.sharding import PartitionSpec as P

DILATION = 16
EPSILON = 1e-05
BF = jnp.bfloat16
F32 = jnp.float32
ROOT_HALF = 0.7071067811865476
PHI_SCALE = 0.3989422804014327
MIB = 1 << 20

WIDE = ("first_gain", "first_shift", "up_bias")
NARROW = ("down_bias", "middle_gain", "middle_shift", "conv_bias", "final_gain", "final_shift")
ROW = {name: row for row, name in enumerate(WIDE + NARROW)}
TABLE_ROWS = 16


def add_up(terms, kind):
    total = terms[0].astype(F32)
    for term in terms[1:]:
        total = total + term.astype(F32)
    return total.astype(kind)


class Grid:
    def __init__(self, seq, batch):
        self.seq, self.batch = seq, batch
        self.side = math.isqrt(seq)
        assert self.side * self.side == seq
        self.depth = batch // 2
        self.half = self.depth // 2

    def here(self):
        s, b = lax.axis_index("seq"), lax.axis_index("batch")
        return s // self.side, s % self.side, b // 2, b % 2

    def send(self, value, move):
        pairs = []
        for s in range(self.seq):
            for b in range(self.batch):
                h, l, z, c = move(s // self.side, s % self.side, b // 2, b % 2)
                pairs.append((s * self.batch + b, (h * self.side + l) * self.batch + z * 2 + c))
        return lax.ppermute(value, ("seq", "batch"), pairs)

    def high(self, value, k):
        return self.send(value, lambda h, l, z, c: ((h + k) % self.side, l, z, c))

    def low(self, value, k):
        return self.send(value, lambda h, l, z, c: (h, (l + k) % self.side, z, c))

    def deep(self, value, k):
        return self.send(value, lambda h, l, z, c: (h, l, (z + k) % self.depth, c))

    def core(self, value):
        return self.send(value, lambda h, l, z, c: (h, l, z, 1 - c))

    def gather_deep(self, piece):
        far = [piece] + [self.deep(piece, k) for k in range(1, self.depth)]
        return jnp.stack(far[: self.half]), jnp.stack(far[self.half :])

    def gather_near(self, one, two):
        one = jnp.stack([one] + [self.low(one, k) for k in range(1, self.side)])
        two = jnp.stack([two] + [self.high(two, k) for k in range(1, self.side)])
        return one, two

    def gather_far(self, one, two):
        one = jnp.stack([one] + [self.high(one, k) for k in range(1, self.side)])
        two = jnp.stack([two] + [self.low(two, k) for k in range(1, self.side)])
        return one, two

    def gather_core(self, one, two):
        return one, two, self.core(one), self.core(two)

    def reduce_core(self, keep_one, keep_two, give_one, give_two):
        return (
            add_up([keep_one, self.core(give_one)], BF),
            add_up([keep_two, self.core(give_two)], BF),
        )

    def reduce_far(self, one, two):
        one = add_up([one[0]] + [self.high(one[k], -k) for k in range(1, self.side)], BF)
        two = add_up([two[0]] + [self.low(two[k], -k) for k in range(1, self.side)], BF)
        return one, two

    def reduce_near(self, one, two):
        one = add_up([one[0]] + [self.low(one[k], -k) for k in range(1, self.side)], BF)
        two = add_up([two[0]] + [self.high(two[k], -k) for k in range(1, self.side)], BF)
        return one, two

    def reduce_deep(self, one, two):
        column = [one[k] for k in range(self.half)] + [two[k] for k in range(self.half)]
        return (column[0],) + tuple(self.deep(column[k], -k) for k in range(1, self.depth))


def near_distance(grid, place, s):
    side = grid.side
    return (
        lax.rem(place[0] - s // side + side, side),
        lax.rem(place[1] - s % side + side, side),
    )


def deep_distance(grid, place, b):
    return lax.rem(place[2] - b // 2 + grid.depth, grid.depth)


def spot_of(grid, place, s, b):
    rh, rl = near_distance(grid, place, s)
    rz = deep_distance(grid, place, b)
    second = rz >= grid.half
    return (
        jnp.where(second, 1, 0),
        jnp.where(second, rl, rh),
        jnp.where(second, rh, rl),
        jnp.where(second, rz - grid.half, rz),
    )


def distance(grid, place, s, b):
    return (jnp.where(place[3] == b % 2, 0, 1),) + spot_of(grid, place, s, b)


class Order:
    def __init__(self, grid, hidden):
        self.grid, self.hidden = grid, hidden
        self.hl, self.hb = hidden // grid.seq, hidden // grid.batch
        self.main = self.hl // 128 * 128
        self.rest = self.hl - self.main

    def runs(self, first, count):
        found = []
        at = first
        while at < first + count:
            block, r = at // self.hl, at % self.hl
            if r < self.main:
                length = min(self.main - r, first + count - at)
                place = block * self.main + r
            else:
                length = min(self.hl - r, first + count - at)
                place = self.grid.seq * self.main + block * self.rest + r - self.main
            if found and found[-1][1] + found[-1][2] == place:
                found[-1] = (found[-1][0], found[-1][1], found[-1][2] + length)
            else:
                found.append((at - first, place, length))
            at += length
        return found


def join(parts):
    return parts[0] if len(parts) == 1 else jnp.concatenate(parts, axis=1)


def wire_from_rows(order, row_blocks):
    main, rest, seq = order.main, order.rest, order.grid.seq
    pieces = []
    for s in range(seq):
        parts = [block[:, s * main : (s + 1) * main] for block in row_blocks if main]
        if rest:
            at = seq * main + s * rest
            parts += [block[:, at : at + rest] for block in row_blocks]
        pieces.append(join(parts))
    return pieces


def rows_from_wire(order, pieces, count, j):
    main, rest = order.main, order.rest
    parts = [piece[:, j * main : (j + 1) * main] for piece in pieces if main]
    if rest:
        at = count * main + j * rest
        parts += [piece[:, at : at + rest] for piece in pieces]
    return join(parts)


def stage_copies(place, parts, stage, sems):
    copies = []
    for index, part in enumerate(parts):
        core = jnp.where(place[3] == 0, index // 2, 1 - index // 2)
        copies.append(
            pltpu.make_async_copy(part, stage.at[core, index % 2], sems.at[index])
        )
    for copy in copies:
        copy.start()
    return copies


def staged(grid, place, stage, s, b):
    return stage[(b % 2,) + spot_of(grid, place, s, b)]


def hand_out(pieces, parts, sems):
    copies = [
        pltpu.make_async_copy(pieces.at[index // 2, index % 2], part, sems.at[index])
        for index, part in enumerate(parts)
    ]
    for copy in copies:
        copy.start()
    for copy in copies:
        copy.wait()


def piece_shape(grid, rows, lanes):
    return (grid.side, grid.side, grid.half, rows, lanes)


def vector_slots(grid, order, model, lanes):
    slots = []
    for b in range(grid.batch):
        at = 0
        for name in WIDE + NARROW:
            if name in WIDE:
                width = model // grid.batch
                runs = [(0, b * width, width)]
            else:
                width = order.hb
                runs = order.runs(b * width, width)
            for offset, spot, length in runs:
                done = 0
                while done < length:
                    flat = at + offset + done
                    take = min(length - done, lanes - flat % lanes)
                    slots.append((ROW[name], flat // lanes, flat % lanes, spot + done, take, b))
                    done += take
            at += width
    return slots


def normed(values):
    center = values - jnp.mean(values, axis=-1, keepdims=True)
    spread = jnp.mean(center * center, axis=-1, keepdims=True)
    inverse = lax.rsqrt(spread + EPSILON)
    return center * inverse, inverse


def cumulative(s):
    return 0.5 + 0.5 * lax.erf(s * ROOT_HALF)


def gelu(s):
    return s * cumulative(s)


def gelu_slope(s):
    return cumulative(s) + s * (PHI_SCALE * jnp.exp(-0.5 * s * s))


def back_rows(q, gain, unit, inverse):
    weighted = q * gain
    first = jnp.mean(weighted, axis=-1, keepdims=True)
    second = jnp.mean(weighted * unit, axis=-1, keepdims=True)
    return (weighted - first - unit * second) * inverse


def row_sum(values):
    return jnp.sum(values, axis=0, keepdims=True)


def dot_nn(left, right):
    return lax.dot_general(left, right, (((1,), (0,)), ((), ())), preferred_element_type=F32)


def dot_nt(left, right):
    return lax.dot_general(left, right, (((1,), (1,)), ((), ())), preferred_element_type=F32)


def dot_tn(left, right):
    return lax.dot_general(left, right, (((0,), (0,)), ((), ())), preferred_element_type=F32)


def params(limit):
    return pltpu.CompilerParams(
        dimension_semantics=("arbitrary",), vmem_limit_bytes=limit * MIB
    )


def cost(flops, bytes_accessed, transcendentals=0):
    return pl.CostEstimate(
        flops=flops, bytes_accessed=bytes_accessed, transcendentals=transcendentals
    )


def whole(shape):
    return pl.BlockSpec(shape, lambda i, *_: (0,) * len(shape))


def rows_of(block):
    return pl.BlockSpec(block, lambda i, *_: (i,) + (0,) * (len(block) - 1))


def sds(shape, kind):
    return jax.ShapeDtypeStruct(shape, kind)


def pack_first_kernel(grid, order, model, down, *refs):
    values, first = refs[:-1], refs[-1]
    hb, dl = order.hb, down.shape[0]
    first[0:hb] = down[...].astype(F32).T.astype(BF)
    sub = lax.broadcasted_iota(jnp.int32, (16, dl), 0)
    tail = jnp.zeros((16, dl), F32)
    at = 0
    for value in values:
        width = value.shape[1]
        done = 0
        while done < width:
            line, column = (at + done) // dl, (at + done) % dl
            take = min(width - done, dl - column)
            tail = tail + jnp.where(
                sub == line, place_in_row(value[:, done : done + take].astype(F32), column, dl), 0.0
            )
            done += take
        at += width
    first[hb : hb + 16] = tail.astype(BF)


def place_in_row(value, column, lanes):
    parts = [value]
    if column:
        parts.insert(0, jnp.zeros((1, column), F32))
    if column + value.shape[1] < lanes:
        parts.append(jnp.zeros((1, lanes - column - value.shape[1]), F32))
    return join(parts)


def pack_first(grid, order, model, down, values):
    hb, dl = order.hb, down.shape[0]
    return pl.pallas_call(
        functools.partial(pack_first_kernel, grid, order, model),
        out_shape=sds((hb + 16, dl), BF),
        compiler_params=pltpu.CompilerParams(vmem_limit_bytes=16 * MIB),
        cost_estimate=cost(0, 4 * hb * dl),
        name="pack_first",
    )(down, *[value.reshape(1, -1) for value in values])


def pack_second_kernel(order, conv, up, second):
    hb, taps = order.hb, conv.shape[0]
    fold = up.shape[1] // hb
    blocks = [conv[k].astype(F32).T.astype(BF) for k in range(taps)]
    turned = up[...].astype(F32).T.astype(BF)
    blocks += [turned[f * hb : (f + 1) * hb] for f in range(fold)]
    parts = [block[:, : order.main] for block in blocks if order.main]
    if order.rest:
        parts += [block[:, order.main :] for block in blocks]
    second[...] = join(parts)


def pack_second(order, conv, up):
    hb = order.hb
    blocks = conv.shape[0] + up.shape[1] // hb
    return pl.pallas_call(
        functools.partial(pack_second_kernel, order),
        out_shape=sds((hb, blocks * order.hl), BF),
        compiler_params=pltpu.CompilerParams(vmem_limit_bytes=16 * MIB),
        cost_estimate=cost(0, 4 * hb * blocks * order.hl),
        name="pack_second",
    )(conv, up)


def unpack_rest_kernel(order, taps, *refs):
    terms, (conv, up) = refs[:-2], refs[-2:]
    hb = order.hb
    fold = up.shape[1] // hb
    total = add_up([term[...] for term in terms], F32)
    for j in range(taps + fold):
        block = rows_from_wire(order, [total], taps + fold, j).T
        if j < taps:
            conv[j] = block
        else:
            up[:, (j - taps) * hb : (j - taps + 1) * hb] = block


def unpack_rest(order, taps, fold, terms):
    return pl.pallas_call(
        functools.partial(unpack_rest_kernel, order, taps),
        out_shape=(
            sds((taps, order.hl, order.hb), F32),
            sds((order.hl, fold * order.hb), F32),
        ),
        compiler_params=pltpu.CompilerParams(vmem_limit_bytes=16 * MIB),
        cost_estimate=cost(0, 8 * (taps + fold) * order.hl * order.hb),
        name="unpack_rest",
    )(*terms)


def unpack_first_kernel(order, *refs):
    terms, (down, tail) = refs[:-2], refs[-2:]
    hb = order.hb
    total = add_up([term[...] for term in terms], F32)
    down[...] = total[0:hb].T
    tail[...] = total[hb : hb + 16]


def unpack_first(order, terms):
    dl = terms[0].shape[1]
    return pl.pallas_call(
        functools.partial(unpack_first_kernel, order),
        out_shape=(sds((dl, order.hb), F32), sds((16, dl), F32)),
        compiler_params=pltpu.CompilerParams(vmem_limit_bytes=16 * MIB),
        cost_estimate=cost(0, 8 * dl * order.hb),
        name="unpack_first",
    )(*terms)


def stage_one_kernel(
    grid, order, place, start_ref, length_ref, tokens, one_m, two_m, one_o, two_o,
    hidden_one, narrow, conv_input, down_t, table, stage, sems,
):
    model = tokens.shape[2]
    hidden = narrow.shape[2]
    hb, dl = order.hb, model // grid.seq

    @pl.when(pl.program_id(0) == 0)
    def _():
        copies = stage_copies(place, (one_m, two_m, one_o, two_o), stage, sems)
        for copy in copies:
            copy.wait()
        table[...] = jnp.zeros_like(table)
        for b in range(grid.batch):
            pieces = [staged(grid, place, stage, s, b) for s in range(grid.seq)]
            block = join([piece[0:hb] for piece in pieces])
            for offset, spot, length in order.runs(b * hb, hb):
                down_t[spot : spot + length] = block[offset : offset + length]
            tail = pieces[0][hb : hb + 16].astype(F32)
            for row, line, column, spot, length, owner in vector_slots(grid, order, model, dl):
                if owner == b:
                    table[row : row + 1, spot : spot + length] = tail[
                        line : line + 1, column : column + length
                    ]

    def vec(name, width):
        return table[ROW[name] : ROW[name] + 1, 0:width]

    unit, _ = normed(tokens[0].astype(F32))
    one = gelu(unit * vec("first_gain", model) + vec("first_shift", model)).astype(BF)
    hidden_one[0] = one
    values = dot_nt(one, down_t[...]) + vec("down_bias", hidden)
    narrow[0] = values
    unit, _ = normed(values)
    active = gelu(unit * vec("middle_gain", hidden) + vec("middle_shift", hidden))
    position = start_ref[0] + lax.broadcasted_iota(jnp.int32, (values.shape[0], 1), 0)
    valid = (position < length_ref[pl.program_id(0)]).astype(F32)
    conv_input[0] = (active * valid).astype(BF)


def stage_one(grid, order, place, start, lengths, tokens, parts):
    count, span, model = tokens.shape
    hidden = order.hidden
    rows, lanes = parts[0].shape[-2:]
    return pl.pallas_call(
        functools.partial(stage_one_kernel, grid, order),
        out_shape=(
            sds((count, span, model), BF),
            sds((count, span, hidden), F32),
            sds((count, span, hidden), BF),
            sds((hidden, model), BF),
            sds((TABLE_ROWS, model), F32),
        ),
        grid_spec=pltpu.PrefetchScalarGridSpec(
            num_scalar_prefetch=3,
            grid=(count,),
            in_specs=[rows_of((1, span, model))]
            + [pl.BlockSpec(memory_space=pl.ANY)] * 4,
            out_specs=[
                rows_of((1, span, model)),
                rows_of((1, span, hidden)),
                rows_of((1, span, hidden)),
                whole((hidden, model)),
                whole((TABLE_ROWS, model)),
            ],
            scratch_shapes=[
                pltpu.VMEM((2, 2) + piece_shape(grid, rows, lanes), BF),
                pltpu.SemaphoreType.DMA((4,)),
            ],
        ),
        compiler_params=params(60),
        cost_estimate=cost(
            2 * count * span * model * hidden, count * span * (4 * model + 6 * hidden)
        ),
        name="stage_one",
    )(place, start, lengths, tokens, *parts)


def fill_padded(padded, left, body, right):
    reach = left.shape[0]
    span = body.shape[0]
    padded[0:reach] = left
    padded[reach : reach + span] = body
    padded[reach + span : 2 * reach + span] = right


def stage_two_kernel(
    grid, order, taps, place, tokens, cotangent, conv_input, left, right, table,
    one_m, two_m, one_o, two_o,
    output, conv_out_grad, sums, part_a, part_b, part_c, part_d, conv_t,
    padded, up_t, total, conv_total, stage, pieces, sems, out_sems,
):
    span, model = tokens.shape[1], tokens.shape[2]
    hidden = conv_input.shape[2]
    hb = order.hb
    fold = model // hidden
    blocks = taps + fold

    def vec(name, width):
        return table[ROW[name] : ROW[name] + 1, 0:width]

    @pl.when(pl.program_id(0) == 0)
    def _():
        copies = stage_copies(place, (one_m, two_m, one_o, two_o), stage, sems)
        sums[...] = jnp.zeros_like(sums)
        total[...] = jnp.zeros_like(total)
        conv_total[...] = jnp.zeros_like(conv_total)
        for copy in copies:
            copy.wait()
        for b in range(grid.batch):
            wires = [staged(grid, place, stage, s, b) for s in range(grid.seq)]
            for k in range(taps):
                block = rows_from_wire(order, wires, blocks, k)
                for offset, spot, length in order.runs(b * hb, hb):
                    conv_t[k, spot : spot + length] = block[offset : offset + length]
            for f in range(fold):
                row = (b * fold + f) * hb
                up_t[row : row + hb] = rows_from_wire(order, wires, blocks, taps + f)

    fill_padded(padded, left[0], conv_input[0], right[0])
    values = dot_nt(padded[0:span], conv_t[0])
    for k in range(1, taps):
        values = values + dot_nt(padded[k * DILATION : k * DILATION + span], conv_t[k])
    values = values + vec("conv_bias", hidden)
    unit, inverse = normed(values)
    gain = vec("final_gain", hidden)
    s = unit * gain + vec("final_shift", hidden)
    phi = cumulative(s)
    three = (s * phi).astype(BF)
    slope = phi + s * (PHI_SCALE * jnp.exp(-0.5 * s * s))
    incoming = cotangent[0]
    result = tokens[0].astype(F32) + dot_nt(three, up_t[...]) + vec("up_bias", model)
    output[0] = result.astype(BF)
    q = dot_nn(incoming, up_t[...]) * slope
    grad = back_rows(q, gain, unit, inverse).astype(BF)
    conv_out_grad[0] = grad

    def add(name, values):
        width = values.shape[1]
        sums[ROW[name] : ROW[name] + 1, 0:width] += row_sum(values)

    add("final_gain", q * unit)
    add("final_shift", q)
    add("conv_bias", grad.astype(F32))
    add("up_bias", incoming.astype(F32))
    total[...] += dot_tn(incoming, three)
    flipped = grad.T
    for k in range(taps):
        conv_total[k] += dot_nn(flipped, padded[k * DILATION : k * DILATION + span])

    @pl.when(pl.program_id(0) == pl.num_programs(0) - 1)
    def _():
        for b in range(grid.batch):
            for offset, spot, length in order.runs(b * hb, hb):
                rows = [conv_total[k, spot : spot + length].astype(BF) for k in range(taps)]
                for f in range(fold):
                    at = (b * fold + f) * hb + offset
                    rows.append(total[at : at + length].astype(BF))
                for s, piece in enumerate(wire_from_rows(order, rows)):
                    pieces[distance(grid, place, s, b) + (pl.ds(offset, length),)] = piece
        hand_out(pieces, (part_a, part_b, part_c, part_d), out_sems)


def stage_two(grid, order, taps, place, tokens, cotangent, conv_input, left, right, table, parts):
    count, span, model = tokens.shape
    hidden = conv_input.shape[2]
    reach = left.shape[1]
    rows, lanes = parts[0].shape[-2:]
    fold = model // hidden
    pieces = piece_shape(grid, order.hb, (taps + fold) * order.hl)
    return pl.pallas_call(
        functools.partial(stage_two_kernel, grid, order, taps),
        out_shape=(
            sds((count, span, model), BF),
            sds((count, span, hidden), BF),
            sds((TABLE_ROWS, model), F32),
            *[sds(pieces, BF)] * 4,
            sds((taps, hidden, hidden), BF),
        ),
        grid_spec=pltpu.PrefetchScalarGridSpec(
            num_scalar_prefetch=1,
            grid=(count,),
            in_specs=[
                rows_of((1, span, model)),
                rows_of((1, span, model)),
                rows_of((1, span, hidden)),
                rows_of((1, reach, hidden)),
                rows_of((1, reach, hidden)),
                whole(table.shape),
            ]
            + [pl.BlockSpec(memory_space=pl.ANY)] * 4,
            out_specs=[
                rows_of((1, span, model)),
                rows_of((1, span, hidden)),
                whole((TABLE_ROWS, model)),
                *[pl.BlockSpec(memory_space=pl.ANY)] * 4,
                whole((taps, hidden, hidden)),
            ],
            scratch_shapes=[
                pltpu.VMEM((span + 2 * reach, hidden), BF),
                pltpu.VMEM((model, hidden), BF),
                pltpu.VMEM((model, hidden), F32),
                pltpu.VMEM((taps, hidden, hidden), F32),
                pltpu.VMEM((2, 2) + piece_shape(grid, rows, lanes), BF),
                pltpu.VMEM((2, 2) + pieces, BF),
                pltpu.SemaphoreType.DMA((4,)),
                pltpu.SemaphoreType.DMA((4,)),
            ],
        ),
        compiler_params=params(60),
        cost_estimate=cost(
            2 * count * span * hidden * (2 * taps * hidden + 3 * model),
            count * span * (6 * model + 4 * hidden),
        ),
        name="stage_two",
    )(place, tokens, cotangent, conv_input, left, right, table, *parts)


def stage_three_kernel(
    start_ref, length_ref, narrow, conv_out_grad, left, right, table, sums_in, conv_t,
    narrow_grad, sums, padded,
):
    span, hidden = narrow.shape[1], narrow.shape[2]
    taps = conv_t.shape[0]

    def vec(name, width):
        return table[ROW[name] : ROW[name] + 1, 0:width]

    def add(name, values):
        width = values.shape[1]
        sums[ROW[name] : ROW[name] + 1, 0:width] += row_sum(values)

    @pl.when(pl.program_id(0) == 0)
    def _():
        sums[...] = sums_in[...]

    fill_padded(padded, left[0], conv_out_grad[0], right[0])
    back = None
    for k in range(taps):
        at = (taps - 1 - k) * DILATION
        term = dot_nn(padded[at : at + span], conv_t[k])
        back = term if back is None else back + term
    position = start_ref[0] + lax.broadcasted_iota(jnp.int32, (span, 1), 0)
    valid = (position < length_ref[pl.program_id(0)]).astype(F32)
    back = back * valid
    unit, inverse = normed(narrow[0])
    gain = vec("middle_gain", hidden)
    q = back * gelu_slope(unit * gain + vec("middle_shift", hidden))
    low = back_rows(q, gain, unit, inverse).astype(BF)
    narrow_grad[0] = low
    add("middle_gain", q * unit)
    add("middle_shift", q)
    add("down_bias", low.astype(F32))


def stage_three(start, lengths, narrow, conv_out_grad, left, right, table, sums, conv_t):
    count, span, hidden = narrow.shape
    taps = conv_t.shape[0]
    reach = left.shape[1]

    return pl.pallas_call(
        stage_three_kernel,
        out_shape=(sds((count, span, hidden), BF), sds(sums.shape, F32)),
        grid_spec=pltpu.PrefetchScalarGridSpec(
            num_scalar_prefetch=2,
            grid=(count,),
            in_specs=[
                rows_of((1, span, hidden)),
                rows_of((1, span, hidden)),
                rows_of((1, reach, hidden)),
                rows_of((1, reach, hidden)),
                whole(table.shape),
                whole(table.shape),
                whole(conv_t.shape),
            ],
            out_specs=[rows_of((1, span, hidden)), whole(sums.shape)],
            scratch_shapes=[pltpu.VMEM((span + 2 * reach, hidden), BF)],
        ),
        compiler_params=params(40),
        cost_estimate=cost(
            2 * count * span * hidden * taps * hidden, count * span * 8 * hidden
        ),
        name="stage_three",
    )(start, lengths, narrow, conv_out_grad, left, right, table, sums, conv_t)


def stage_four_kernel(
    grid, order, last, begin, place, tokens, cotangent, hidden_one, narrow_grad, table, sums_in,
    down_t, *refs,
):
    if begin:
        grad_in, total_in = None, None
    else:
        grad_in, total_in, refs = refs[0], refs[1], refs[2:]
    tokens_grad, sums, total = refs[:3]
    model = tokens.shape[2]
    hidden = narrow_grad.shape[2]
    hb, dl = order.hb, model // grid.seq

    def vec(name, width):
        return table[ROW[name] : ROW[name] + 1, 0:width]

    def add(name, values):
        width = values.shape[1]
        sums[ROW[name] : ROW[name] + 1, 0:width] += row_sum(values)

    @pl.when(pl.program_id(0) == 0)
    def _():
        sums[...] = sums_in[...]
        total[...] = jnp.zeros_like(total) if begin else total_in[...]

    low = narrow_grad[0]
    total[...] += dot_tn(low, hidden_one[0])
    deep = dot_nn(low, down_t[...])
    unit, inverse = normed(tokens[0].astype(F32))
    gain = vec("first_gain", model)
    q = deep * gelu_slope(unit * gain + vec("first_shift", model))
    add("first_gain", q * unit)
    add("first_shift", q)
    grad = back_rows(q, gain, unit, inverse) + cotangent[0].astype(F32)
    tokens_grad[0] = grad.astype(BF)

    if last:
        part_a, part_b, part_c, part_d, pieces, out_sems = refs[3:]

        @pl.when(pl.program_id(0) == pl.num_programs(0) - 1)
        def _():
            sub = lax.broadcasted_iota(jnp.int32, (16, dl), 0)
            for b in range(grid.batch):
                tail = jnp.zeros((16, dl), F32)
                for row, line, column, spot, length, owner in vector_slots(grid, order, model, dl):
                    if owner != b:
                        continue
                    parts = [sums[row : row + 1, spot : spot + length]]
                    if column:
                        parts.insert(0, jnp.zeros((1, column), F32))
                    if column + length < dl:
                        parts.append(jnp.zeros((1, dl - column - length), F32))
                    tail = tail + jnp.where(sub == line, join(parts), 0.0)
                tail = tail.astype(BF)
                for s in range(grid.seq):
                    to = distance(grid, place, s, b)
                    for offset, spot, length in order.runs(b * hb, hb):
                        pieces[to + (pl.ds(offset, length),)] = total[
                            spot : spot + length, s * dl : (s + 1) * dl
                        ].astype(BF)
                    pieces[to + (pl.ds(hb, 16),)] = tail
            hand_out(pieces, (part_a, part_b, part_c, part_d), out_sems)


def stage_four(
    grid, order, first, part, begin, last, place, tokens, cotangent, hidden_one, narrow_grad,
    table, sums, down_t, grad_in, total_in,
):
    count, span, model = tokens.shape
    hidden = narrow_grad.shape[2]
    pieces = piece_shape(grid, order.hb + 16, model // grid.seq)

    def part_of(block):
        return pl.BlockSpec(block, lambda i, *_: (first + i,) + (0,) * (len(block) - 1))

    in_specs = [
        part_of((1, span, model)),
        part_of((1, span, model)),
        part_of((1, span, model)),
        part_of((1, span, hidden)),
        whole(table.shape),
        whole(table.shape),
        whole(down_t.shape),
    ]
    inputs = [tokens, cotangent, hidden_one, narrow_grad, table, sums, down_t]
    aliases = {}
    if not begin:
        in_specs += [pl.BlockSpec(memory_space=pl.ANY), whole((hidden, model))]
        inputs += [grad_in, total_in]
        aliases = {8: 0}
    out_shape = [
        sds((count, span, model), BF),
        sds(table.shape, F32),
        sds((hidden, model), F32),
    ]
    out_specs = [part_of((1, span, model)), whole(table.shape), whole((hidden, model))]
    scratch = []
    if last:
        out_shape += [sds(pieces, BF)] * 4
        out_specs += [pl.BlockSpec(memory_space=pl.ANY)] * 4
        scratch = [pltpu.VMEM((2, 2) + pieces, BF), pltpu.SemaphoreType.DMA((4,))]
    return pl.pallas_call(
        functools.partial(stage_four_kernel, grid, order, last, begin),
        out_shape=tuple(out_shape),
        grid_spec=pltpu.PrefetchScalarGridSpec(
            num_scalar_prefetch=1,
            grid=(part,),
            in_specs=in_specs,
            out_specs=out_specs,
            scratch_shapes=scratch,
        ),
        input_output_aliases=aliases,
        compiler_params=params(48),
        cost_estimate=cost(
            4 * part * span * hidden * model, part * span * (8 * model + 2 * hidden)
        ),
        name="stage_four",
    )(place, *inputs)


def halos(cells, reach):
    count = lax.axis_size("seq")
    left = lax.ppermute(
        cells[:, cells.shape[1] - reach :], "seq", [(i, i + 1) for i in range(count - 1)]
    )
    right = lax.ppermute(cells[:, :reach], "seq", [(i + 1, i) for i in range(count - 1)])
    return left, right


def after(value, *others):
    return lax.optimization_barrier((value,) + others)[0]


def body(
    grid,
    tokens,
    lengths,
    first_gain,
    first_shift,
    down_weight,
    down_bias,
    middle_gain,
    middle_shift,
    conv_weight,
    conv_bias,
    final_gain,
    final_shift,
    up_weight,
    up_bias,
    cotangent,
):
    shape = tokens.shape
    span, model = shape[2], shape[3]
    count = shape[0] * shape[1]
    taps = conv_weight.shape[0]
    hidden = down_weight.shape[1] * grid.batch
    order = Order(grid, hidden)
    hb, hl, dl = order.hb, order.hl, down_weight.shape[0]
    fold = model // hidden
    reach = (taps - 1) // 2 * DILATION

    tokens = tokens.reshape(count, span, model)
    cotangent = cotangent.reshape(count, span, model)
    lengths = lengths.reshape(count)
    place = jnp.stack(grid.here()).astype(jnp.int32)
    start = (lax.axis_index("seq") * span).astype(jnp.int32).reshape(1)

    vectors = {
        "first_gain": first_gain,
        "first_shift": first_shift,
        "up_bias": up_bias,
        "down_bias": down_bias,
        "middle_gain": middle_gain,
        "middle_shift": middle_shift,
        "conv_bias": conv_bias,
        "final_gain": final_gain,
        "final_shift": final_shift,
    }
    first_piece = pack_first(
        grid, order, model, down_weight, [vectors[name] for name in WIDE + NARROW]
    )
    second_piece = pack_second(order, after(conv_weight, first_piece), up_weight)

    def meet(*groups):
        flat = lax.optimization_barrier(tuple(value for group in groups for value in group))
        found, at = [], 0
        for group in groups:
            found.append(flat[at : at + len(group)])
            at += len(group)
        return found

    first = grid.gather_deep(first_piece)
    first = grid.gather_near(*first)
    first, (second_piece,) = meet(first, (second_piece,))
    second = grid.gather_deep(second_piece)
    first = grid.gather_far(*first)
    second, first = meet(second, first)
    second = grid.gather_near(*second)
    first = grid.gather_core(*first)
    second, first = meet(second, first)
    second = grid.gather_far(*second)
    hidden_one, narrow, conv_input, down_t, table = stage_one(
        grid, order, place, start, lengths, tokens, first
    )
    second, (conv_input,) = meet(second, (conv_input,))
    left, right = halos(conv_input, reach)
    second = grid.gather_core(*second)
    block_output, conv_out_grad, sums, *rest, conv_t = stage_two(
        grid, order, taps, place, tokens, cotangent, conv_input, left, right, table, second
    )
    half = count // 2

    left, right = halos(conv_out_grad, reach)
    rest = grid.reduce_core(*rest)
    rest, (sums, left, right) = meet(rest, (sums, left, right))

    rest = grid.reduce_far(*rest)
    narrow_grad, sums = stage_three(
        start, lengths, narrow, conv_out_grad, left, right, table, sums, conv_t
    )
    rest, (sums,) = meet(rest, (sums,))

    rest = grid.reduce_near(*rest)
    tokens_grad, sums, total = stage_four(
        grid, order, 0, half, True, False, place, tokens, cotangent, hidden_one, narrow_grad,
        table, sums, down_t, None, None,
    )
    rest, (sums,) = meet(rest, (sums,))

    rest = grid.reduce_deep(*rest)
    tokens_grad, sums, total, *down = stage_four(
        grid, order, half, half, False, True, place, tokens, cotangent, hidden_one, narrow_grad,
        table, sums, down_t, tokens_grad, total,
    )
    rest, down = meet(rest, down)

    down = grid.reduce_near(*grid.reduce_far(*grid.reduce_core(*down)))
    down = grid.reduce_deep(*down)
    conv_grad, up_grad = unpack_rest(order, taps, fold, rest)
    down_grad, tail = unpack_first(order, down)
    tail = tail.reshape(-1)
    grads = {}
    at = 0
    for name in WIDE + NARROW:
        width = vectors[name].shape[0]
        grads[name] = tail[at : at + width]
        at += width
    return (
        block_output.reshape(shape),
        tokens_grad.reshape(shape),
        grads["first_gain"],
        grads["first_shift"],
        down_grad,
        grads["down_bias"],
        grads["middle_gain"],
        grads["middle_shift"],
        conv_grad,
        grads["conv_bias"],
        grads["final_gain"],
        grads["final_shift"],
        up_grad,
        grads["up_bias"],
    )


def solution(mesh):
    grid = Grid(mesh.shape["seq"], mesh.shape["batch"])
    return jax.shard_map(
        functools.partial(body, grid),
        mesh=mesh,
        in_specs=(
            P(None, "batch", "seq", None),
            P(None, "batch"),
            P("batch"),
            P("batch"),
            P("seq", "batch"),
            P("batch"),
            P("batch"),
            P("batch"),
            P(None, "seq", "batch"),
            P("batch"),
            P("batch"),
            P("batch"),
            P("seq", "batch"),
            P("batch"),
            P(None, "batch", "seq", None),
        ),
        out_specs=(
            P(None, "batch", "seq", None),
            P(None, "batch", "seq", None),
            P("batch"),
            P("batch"),
            P("seq", "batch"),
            P("batch"),
            P("batch"),
            P("batch"),
            P(None, "seq", "batch"),
            P("batch"),
            P("batch"),
            P("batch"),
            P("seq", "batch"),
            P("batch"),
        ),
        check_vma=False,
    )
```

time: 327 us -> 255 us (0.78)
  waiting for transfers between devices: 93.7 us -> 53.1 us
  other arithmetic: 19.9 us -> 4.9 us
  local copies, waits for them, and re-layouts: 26.2 us -> 16.9 us
  starting transfers between devices: 65.4 us -> 60.5 us
    ppermute x40 -> x36, waiting for transfers between devices: 93.7 us -> 41.7 us  [send(): return lax.ppermute(value, ('seq', 'batch'), pairs)]
    another operation x15 -> x13, other arithmetic: 12.7 us -> 1.63 us  [the longest x1 0.59 us: body(): place = jnp.stack(grid.here()).astype(jnp.int32)]
    ppermute x2, waiting for transfers between devices: 0.01 us -> 10.5 us  [halos(): lax.ppermute(cells[:, :reach], 'seq', [(i + 1, i) for i in range(count -...]
    ppermute x40 -> x36, starting transfers between devices: 54.6 us -> 45 us  [send(): return lax.ppermute(value, ('seq', 'batch'), pairs)]
    slice x4 -> x0, local copies, waits for them, and re-layouts: 5.95 us -> none  [the longest x3 5.94 us: scatter(): total = add([pieces[0], self.core(pieces[1])], BF)]
    ppermute x2, starting transfers between devices: 7.87 us -> 12.9 us  [halos(): lax.ppermute(cells[:, cells.shape[1] - reach:], 'seq', [(i, i + 1) for i...]
    unnamed x66 -> x56, local copies, waits for them, and re-layouts: 6.55 us -> 10.3 us
    squeeze x19 -> x12, local copies, waits for them, and re-layouts: 3.74 us -> 0.36 us  [the longest x2 0.09 us: reduce_far(): two[k]]
  transfers between devices with their start and end apart: 44 -> 40, of which waited for: 23 -> 20; matrix products, arithmetic and copies ran while one was open for 8% -> 3% of each run, Pallas kernels for 25% -> 25%
where the time goes in v2:
time: 255 us
  Pallas kernels  118 us (46%)
  starting transfers between devices  60.5 us (24%)
  waiting for transfers between devices  53.1 us (21%)
  local copies, waits for them, and re-layouts  16.9 us (7%)
  other arithmetic  4.9 us (2%)
    pallas_call x1, Pallas kernels, stage_two(): pl.pallas_call(functools.partial(stage_two_kernel, grid, order, taps), ou...  54.1 us
    ppermute x36, starting transfers between devices, send(): return lax.ppermute(value, ('seq', 'batch'), pairs)  45 us
    ppermute x36, waiting for transfers between devices, send(): return lax.ppermute(value, ('seq', 'batch'), pairs)  41.7 us
    pallas_call x2, Pallas kernels, stage_four(): pl.pallas_call(functools.partial(stage_four_kernel, grid, order, last, be...  27 us
    pallas_call x1, Pallas kernels, stage_three(): pl.pallas_call(stage_three_kernel, out_shape=(sds((count, span, hidden),...  18.7 us
    pallas_call x1, Pallas kernels, stage_one(): pl.pallas_call(functools.partial(stage_one_kernel, grid, order), out_shap...  16.6 us
    ppermute x2, starting transfers between devices, halos(): lax.ppermute(cells[:, cells.shape[1] - reach:], 'seq', [(i, i + 1) for i...  12.9 us
    ppermute x2, waiting for transfers between devices, halos(): lax.ppermute(cells[:, :reach], 'seq', [(i + 1, i) for i in range(count -...  10.5 us
  transfers between devices with their start and end apart: 40, of which 20 were waited for; matrix products, arithmetic and copies ran while one was open for 3% of the time, Pallas kernels for 25%

profile of v2, /device:TPU:0, one launch (start us, length us, event | category | flops | bytes accessed | tf_op | source)
XLA Modules:
  0.0 254.6 jit_solution(6774054285881155149)
XLA Ops:
  7.6 5.1 %collective-permute-start.3 = (bf16[96,320]{1,0:T(8,128)(2,1)S(1)}, bf16[96,320]{1,0:T(8,128)(2,1)S(1)}, u32[]{:S(2)}, u32[]{:S(2)}) collective-permute-start(bf16[96,320]{1,0:T(8,128)(2,1)S(1)} %pack_first.1), channel_id=1, source_target_pairs={{0,6},{1,7},{2,0},{3,1},{4,2},{5,3},{6,4},{7,5},{8,14},{9,15},{10,... | collective-permute-start | bytes 184328 | tf_op jit(solution)/shard_map/ppermute | solution.py:50
  15.4 4.3 %collective-permute-done.2 = bf16[96,320]{1,0:T(8,128)(2,1)S(1)} collective-permute-done((bf16[96,320]{1,0:T(8,128)(2,1)S(1)}, bf16[96,320]{1,0:T(8,128)(2,1)S(1)}, u32[]{:S(2)}, u32[]{:S(2)}) %collective-permute-start.2) | collective-permute-done | bytes 61472 | tf_op jit(solution)/shard_map/ppermute | solution.py:50
  26.9 1.8 collective-permute-start.7
  32.1 1.8 collective-permute-done.7
  33.8 8.8 %collective-permute-done.6 = bf16[80,1120]{1,0:T(8,128)(2,1)S(1)} collective-permute-done((bf16[80,1120]{1,0:T(8,128)(2,1)S(1)}, bf16[80,1120]{1,0:T(8,128)(2,1)S(1)}, u32[]{:S(2)}, u32[]{:S(2)}) %collective-permute-start.6) | collective-permute-done | bytes 179232 | tf_op jit(solution)/shard_map/ppermute | solution.py:50
  46.2 6.0 %collective-permute-done.10 = bf16[2,80,1120]{2,1,0:T(8,128)(2,1)S(1)} collective-permute-done((bf16[2,80,1120]{2,1,0:T(8,128)(2,1)S(1)}, bf16[2,80,1120]{2,1,0:T(8,128)(2,1)S(1)}, u32[]{:S(2)}, u32[]{:S(2)}) %collective-permute-start.10) | collective-permute-done | bytes 358432 | tf_op jit(solution)/shard_map/ppermute | solution.py:50
  55.6 16.6 %stage_one.1 = (bf16[8,256,1280]{2,1,0:T(8,128)(2,1)}, f32[8,256,640]{2,1,0:T(8,128)}, bf16[8,256,640]{2,1,0:T(8,128)(2,1)}, bf16[640,1280]{1,0:T(8,128)(2,1)}, f32[16,1280]{1,0:T(8,128)}) custom-call(s32[4]{0:T(128)} %pad_add_fusion.place, s32[1]{0:T(128)} %bitcast.36.start_ref, s32[8]{0:T(128)} %reshape.104.length_ref, bf16[8,256,1280]{2,1,0:T(8,128)(2,1)} %bitcast.113, ...), custom_call_target="tpu_custom_call" | custom-call | flops 3355443200 | bytes 18350080 | tf_op jit(solution)/shard_map/stage_one/pallas_call | solution.py:455
  76.5 4.7 %collective-permute-start.16 = (bf16[8,32,640]{2,1,0:T(8,128)(2,1)S(1)}, bf16[8,32,640]{2,1,0:T(8,128)(2,1)S(1)}, u32[]{:S(2)}, u32[]{:S(2)}) collective-permute-start(bf16[8,32,640]{2,1,0:T(8,128)(2,1)S(1)} %get-tuple-element.157), channel_id=1, source_target_pairs={{0,8},{8,16},{16,24},{1,9},{9,17},{17,25},{2,10},{10,18},{18,26},{... | collective-permute-start | bytes 983048 | tf_op jit(solution)/shard_map/ppermute | solution.py:819
  81.2 6.4 %collective-permute-done.17.right = bf16[8,32,640]{2,1,0:T(8,128)(2,1)S(1)} collective-permute-done((bf16[8,32,640]{2,1,0:T(8,128)(2,1)S(1)}, bf16[8,32,640]{2,1,0:T(8,128)(2,1)S(1)}, u32[]{:S(2)}, u32[]{:S(2)}) %collective-permute-start.17) | collective-permute-done | bytes 327712 | tf_op jit(solution)/shard_map/ppermute | solution.py:822
  89.6 54.1 %stage_two.1 = (bf16[8,256,1280]{2,1,0:T(8,128)(2,1)}, bf16[8,256,640]{2,1,0:T(8,128)(2,1)}, f32[16,1280]{1,0:T(8,128)}, bf16[2,2,2,80,1120]{4,3,2,1,0:T(8,128)(...) custom-call(s32[4]{0:T(128)} %pad_add_fusion.place, ...), custom_call_target="tpu_custom_call" | custom-call | flops 26843545600 | bytes 20971520 | tf_op jit(solution)/shard_map/stage_two/pallas_call | solution.py:581
  146.7 8.2 %collective-permute-start.22 = (bf16[8,32,640]{2,1,0:T(8,128)(2,1)S(1)}, bf16[8,32,640]{2,1,0:T(8,128)(2,1)S(1)}, u32[]{:S(2)}, u32[]{:S(2)}) collective-permute-start(bf16[8,32,640]{2,1,0:T(8,128)(2,1)S(1)} %get-tuple-element.155), channel_id=1, source_target_pairs={{0,8},{8,16},{16,24},{1,9},{9,17},{17,25},{2,10},{10,18},{18,26},{... | collective-permute-start | bytes 983048 | tf_op jit(solution)/shard_map/ppermute | solution.py:819
  154.9 1.8 add_convert_fusion.1
  157.1 4.1 %collective-permute-done.23.right = bf16[8,32,640]{2,1,0:T(8,128)(2,1)S(1)} collective-permute-done((bf16[8,32,640]{2,1,0:T(8,128)(2,1)S(1)}, bf16[8,32,640]{2,1,0:T(8,128)(2,1)S(1)}, u32[]{:S(2)}, u32[]{:S(2)}) %collective-permute-start.23) | collective-permute-done | bytes 327712 | tf_op jit(solution)/shard_map/ppermute | solution.py:822
  162.0 5.5 %collective-permute-start.25 = (bf16[2,2,80,1120]{3,2,1,0:T(8,128)(2,1)S(1)}, bf16[2,2,80,1120]{3,2,1,0:T(8,128)(2,1)S(1)}, u32[]{:S(2)}, u32[]{:S(2)}) collective-permute-start(bf16[2,2,80,1120]{3,2,1,0:T(8,128)(2,1)S(1)} %slice_bitcast_fusion), channel_id=1, source_target_pairs={{0,8},{1,9},{2,10},{3,11},{4,12},{5,13},{6,14},{7,15},{8,0},{9,1},... | collective-permute-start | bytes 2150408 | tf_op jit(solution)/shard_map/ppermute | solution.py:50
  167.4 4.4 %collective-permute-start.24 = (bf16[2,2,80,1120]{3,2,1,0:T(8,128)(2,1)S(1)}, bf16[2,2,80,1120]{3,2,1,0:T(8,128)(2,1)S(1)}, u32[]{:S(2)}, u32[]{:S(2)}) collective-permute-start(bf16[2,2,80,1120]{3,2,1,0:T(8,128)(2,1)S(1)} %slice_bitcast_fusion.1), channel_id=1, source_target_pairs={{0,16},{1,17},{2,18},{3,19},{4,20},{5,21},{6,22},{7,23},{8,24},{9,... | collective-permute-start | bytes 2150408 | tf_op jit(solution)/shard_map/ppermute | solution.py:50
  171.9 18.7 %stage_three.1 = (bf16[8,256,640]{2,1,0:T(8,128)(2,1)S(1)}, f32[16,1280]{1,0:T(8,128)S(1)}) custom-call(s32[1]{0:T(128)} %bitcast.36.start_ref, s32[8]{0:T(128)S(1)} %copy-done.13, f32[8,256,640]{2,1,0:T(8,128)} %get-tuple-element.98.narrow, bf16[8,256,640]{2,1,0:T(8,128)(2,1)S(1)} %copy-done.4, bf16[8,32,640]{2,1,0:T(8,128)(2,1)S(1)} %collective-permute-done.22.left, ...), custom_call_target="tpu_custom_call" | custom-call | flops 8388608000 | bytes 10485760 | tf_op jit(solution)/shard_map/stage_three/pallas_call | solution.py:671
  193.0 11.7 %stage_four.2 = (bf16[8,256,1280]{2,1,0:T(8,128)(2,1)}, f32[16,1280]{1,0:T(8,128)S(1)}, f32[640,1280]{1,0:T(8,128)}) custom-call(s32[4]{0:T(128)S(1)} %copy-done.6, bf16[8,256,1280]{2,1,0:T(8,128)(2,1)} %bitcast.115, bf16[8,256,1280]{2,1,0:T(8,128)(2,1)} %bitcast.118, bf16[8,256,1280]{2,1,0:T(8,128)(2,1)} %get-tuple-element.97.hidden_one, ...), custom_call_target="tpu_custom_call" | custom-call | flops 3355443200 | bytes 11796480 | tf_op jit(solution)/shard_map/stage_four/pallas_call | solution.py:798
  207.5 3.9 %collective-permute-start.29 = (bf16[80,1120]{1,0:T(8,128)(2,1)S(1)}, bf16[80,1120]{1,0:T(8,128)(2,1)S(1)}, u32[]{:S(2)}, u32[]{:S(2)}) collective-permute-start(bf16[80,1120]{1,0:T(8,128)(2,1)S(1)} %get-tuple-element.159), channel_id=1, source_target_pairs={{0,4},{1,5},{2,6},{3,7},{4,0},{5,1},{6,2},{7,3},{8,12},{9,13},{10,... | collective-permute-start | bytes 537608 | tf_op jit(solution)/shard_map/ppermute | solution.py:50
  211.4 15.3 %stage_four.3 = (bf16[8,256,1280]{2,1,0:T(8,128)(2,1)}, f32[16,1280]{1,0:T(8,128)}, f32[640,1280]{1,0:T(8,128)}, bf16[2,2,2,96,320]{4,3,2,1,0:T(8,128)(2,1)S(1)}...) custom-call(s32[4]{0:T(128)S(1)} %copy-done.6, ...), custom_call_target="tpu_custom_call", output_to_operand_aliasing={{0}: (8, {})} | custom-call | flops 3355443200 | bytes 11796480 | tf_op jit(solution)/shard_map/stage_four/pallas_call | solution.py:798
  229.9 1.8 collective-permute-start.36
  231.7 6.5 %collective-permute-done.32 = bf16[2,2,96,320]{3,2,1,0:T(8,128)(2,1)S(1)} collective-permute-done((bf16[2,2,96,320]{3,2,1,0:T(8,128)(2,1)S(1)}, bf16[2,2,96,320]{3,2,1,0:T(8,128)(2,1)S(1)}, u32[]{:S(2)}, u32[]{:S(2)}) %collective-permute-start.32) | collective-permute-done | bytes 245792 | tf_op jit(solution)/shard_map/ppermute | solution.py:50
  240.9 2.7 %collective-permute-done.33 = bf16[2,96,320]{2,1,0:T(8,128)(2,1)S(1)} collective-permute-done((bf16[2,96,320]{2,1,0:T(8,128)(2,1)S(1)}, bf16[2,96,320]{2,1,0:T(8,128)(2,1)S(1)}, u32[]{:S(2)}, u32[]{:S(2)}) %collective-permute-start.33) | collective-permute-done | bytes 122912 | tf_op jit(solution)/shard_map/ppermute | solution.py:50
  247.1 1.8 collective-permute-done.34.refs_1_
  248.9 2.0 collective-permute-done.39.refs_3_
  (167 shorter events, 55.5 us)
Async XLA Ops:
  28.7 13.9 %collective-permute-start.6 = (bf16[80,1120]{1,0:T(8,128)(2,1)S(1)}, bf16[80,1120]{1,0:T(8,128)(2,1)S(1)}, u32[]{:S(2)}, u32[]{:S(2)}) collective-permute-start(bf16[80,1120]{1,0:T(8,128)(2,1)S(1)} %pack_second.1), channel_id=1, source_target_pairs={{0,4},{1,5},{2,6},{3,7},{4,0},{5,1},{6,2},{7,3},{8,12},{9,13},{10,... | collective-permute-start | bytes 537608 | tf_op jit(solution)/shard_map/ppermute | solution.py:50
  28.7 13.9 %collective-permute-start.5 = (bf16[80,1120]{1,0:T(8,128)(2,1)S(1)}, bf16[80,1120]{1,0:T(8,128)(2,1)S(1)}, u32[]{:S(2)}, u32[]{:S(2)}) collective-permute-start(bf16[80,1120]{1,0:T(8,128)(2,1)S(1)} %pack_second.1), channel_id=1, source_target_pairs={{0,2},{1,3},{2,4},{3,5},{4,6},{5,7},{6,0},{7,1},{8,10},{9,11},{10,... | collective-permute-start | bytes 537608 | tf_op jit(solution)/shard_map/ppermute | solution.py:50
  29.4 13.3 %collective-permute-start.8 = (bf16[2,2,96,320]{3,2,1,0:T(8,128)(2,1)S(1)}, bf16[2,2,96,320]{3,2,1,0:T(8,128)(2,1)S(1)}, u32[]{:S(2)}, u32[]{:S(2)}) collective-permute-start(bf16[2,2,96,320]{3,2,1,0:T(8,128)(2,1)S(1)} %pad_maximum_fusion.8), channel_id=1, source_target_pairs={{0,16},{1,17},{2,18},{3,19},{4,20},{5,21},{6,22},{7,23},{8,24},{9,... | collective-permute-start | bytes 737288 | tf_op jit(solution)/shard_map/ppermute | solution.py:50
  30.6 12.3 %collective-permute-start.9 = (bf16[2,2,96,320]{3,2,1,0:T(8,128)(2,1)S(1)}, bf16[2,2,96,320]{3,2,1,0:T(8,128)(2,1)S(1)}, u32[]{:S(2)}, u32[]{:S(2)}) collective-permute-start(bf16[2,2,96,320]{3,2,1,0:T(8,128)(2,1)S(1)} %pad_maximum_fusion.9), channel_id=1, source_target_pairs={{0,8},{1,9},{2,10},{3,11},{4,12},{5,13},{6,14},{7,15},{8,0},{9,1},... | collective-permute-start | bytes 737288 | tf_op jit(solution)/shard_map/ppermute | solution.py:50
  43.0 9.2 %collective-permute-start.10 = (bf16[2,80,1120]{2,1,0:T(8,128)(2,1)S(1)}, bf16[2,80,1120]{2,1,0:T(8,128)(2,1)S(1)}, u32[]{:S(2)}, u32[]{:S(2)}) collective-permute-start(bf16[2,80,1120]{2,1,0:T(8,128)(2,1)S(1)} %pad_maximum_fusion.6), channel_id=1, source_target_pairs={{0,8},{1,9},{2,10},{3,11},{4,12},{5,13},{6,14},{7,15},{8,0},{9,1},... | collective-permute-start | bytes 1075208 | tf_op jit(solution)/shard_map/ppermute | solution.py:50
  53.5 18.7 %collective-permute-start.14 = (bf16[2,2,80,1120]{3,2,1,0:T(8,128)(2,1)S(1)}, bf16[2,2,80,1120]{3,2,1,0:T(8,128)(2,1)S(1)}, u32[]{:S(2)}, u32[]{:S(2)}) collective-permute-start(bf16[2,2,80,1120]{3,2,1,0:T(8,128)(2,1)S(1)} %pad_maximum_fusion.2), channel_id=1, source_target_pairs={{0,16},{1,17},{2,18},{3,19},{4,20},{5,21},{6,22},{7,23},{8,24},{9,... | collective-permute-start | bytes 2150408 | tf_op jit(solution)/shard_map/ppermute | solution.py:50
  54.5 17.9 %collective-permute-start.15 = (bf16[2,2,80,1120]{3,2,1,0:T(8,128)(2,1)S(1)}, bf16[2,2,80,1120]{3,2,1,0:T(8,128)(2,1)S(1)}, u32[]{:S(2)}, u32[]{:S(2)}) collective-permute-start(bf16[2,2,80,1120]{3,2,1,0:T(8,128)(2,1)S(1)} %pad_maximum_fusion.3), channel_id=1, source_target_pairs={{0,8},{1,9},{2,10},{3,11},{4,12},{5,13},{6,14},{7,15},{8,0},{9,1},... | collective-permute-start | bytes 2150408 | tf_op jit(solution)/shard_map/ppermute | solution.py:50
  73.5 14.3 %collective-permute-start.18 = (bf16[2,2,2,80,1120]{4,3,2,1,0:T(8,128)(2,1)S(1)}, bf16[2,2,2,80,1120]{4,3,2,1,0:T(8,128)(2,1)S(1)}, u32[]{:S(2)}, u32[]{:S(2)}) collective-permute-start(bf16[2,2,2,80,1120]{4,3,2,1,0:T(8,128)(2,1)S(1)} %pad_maximum_fusion.one_m), channel_id=1, source_target_pairs={{0,1},{1,0},{2,3},{3,2},{4,5},{5,4},{6,7},{7,6},{8,9},{9,8},{10,11... | collective-permute-start | bytes 4300808 | tf_op jit(solution)/shard_map/ppermute | solution.py:50
  73.5 14.4 %collective-permute-start.19 = (bf16[2,2,2,80,1120]{4,3,2,1,0:T(8,128)(2,1)S(1)}, bf16[2,2,2,80,1120]{4,3,2,1,0:T(8,128)(2,1)S(1)}, u32[]{:S(2)}, u32[]{:S(2)}) collective-permute-start(bf16[2,2,2,80,1120]{4,3,2,1,0:T(8,128)(2,1)S(1)} %pad_maximum_fusion.1.two_m), channel_id=1, source_target_pairs={{0,1},{1,0},{2,3},{3,2},{4,5},{5,4},{6,7},{7,6},{8,9},{9,8},{10,11... | collective-permute-start | bytes 4300808 | tf_op jit(solution)/shard_map/ppermute | solution.py:50
  75.2 12.5 %collective-permute-start.17 = (bf16[8,32,640]{2,1,0:T(8,128)(2,1)S(1)}, bf16[8,32,640]{2,1,0:T(8,128)(2,1)S(1)}, u32[]{:S(2)}, u32[]{:S(2)}) collective-permute-start(bf16[8,32,640]{2,1,0:T(8,128)(2,1)S(1)} %get-tuple-element.156), channel_id=1, source_target_pairs={{8,0},{16,8},{24,16},{9,1},{17,9},{25,17},{10,2},{18,10},{26,18},{... | collective-permute-start | bytes 983048 | tf_op jit(solution)/shard_map/ppermute | solution.py:822
  76.5 11.4 %collective-permute-start.16 = (bf16[8,32,640]{2,1,0:T(8,128)(2,1)S(1)}, bf16[8,32,640]{2,1,0:T(8,128)(2,1)S(1)}, u32[]{:S(2)}, u32[]{:S(2)}) collective-permute-start(bf16[8,32,640]{2,1,0:T(8,128)(2,1)S(1)} %get-tuple-element.157), channel_id=1, source_target_pairs={{0,8},{8,16},{16,24},{1,9},{9,17},{17,25},{2,10},{10,18},{18,26},{... | collective-permute-start | bytes 983048 | tf_op jit(solution)/shard_map/ppermute | solution.py:819
  143.7 11.2 %collective-permute-start.20 = (bf16[2,2,2,80,1120]{4,3,2,1,0:T(8,128)(2,1)}, bf16[2,2,2,80,1120]{4,3,2,1,0:T(8,128)(2,1)S(1)}, u32[]{:S(2)}, u32[]{:S(2)}) collective-permute-start(bf16[2,2,2,80,1120]{4,3,2,1,0:T(8,128)(2,1)} %get-tuple-element.101), channel_id=1, source_target_pairs={{0,1},{1,0},{2,3},{3,2},{4,5},{5,4},{6,7},{7,6},{8,9},{9,8},{10,11... | collective-permute-start | bytes 4300808 | tf_op jit(solution)/shard_map/ppermute | solution.py:50
  143.8 13.0 %collective-permute-start.21 = (bf16[2,2,2,80,1120]{4,3,2,1,0:T(8,128)(2,1)}, bf16[2,2,2,80,1120]{4,3,2,1,0:T(8,128)(2,1)S(1)}, u32[]{:S(2)}, u32[]{:S(2)}) collective-permute-start(bf16[2,2,2,80,1120]{4,3,2,1,0:T(8,128)(2,1)} %get-tuple-element.103), channel_id=1, source_target_pairs={{0,1},{1,0},{2,3},{3,2},{4,5},{5,4},{6,7},{7,6},{8,9},{9,8},{10,11... | collective-permute-start | bytes 4300808 | tf_op jit(solution)/shard_map/ppermute | solution.py:50
  145.4 15.8 %collective-permute-start.23 = (bf16[8,32,640]{2,1,0:T(8,128)(2,1)S(1)}, bf16[8,32,640]{2,1,0:T(8,128)(2,1)S(1)}, u32[]{:S(2)}, u32[]{:S(2)}) collective-permute-start(bf16[8,32,640]{2,1,0:T(8,128)(2,1)S(1)} %get-tuple-element.154), channel_id=1, source_target_pairs={{8,0},{16,8},{24,16},{9,1},{17,9},{25,17},{10,2},{18,10},{26,18},{... | collective-permute-start | bytes 983048 | tf_op jit(solution)/shard_map/ppermute | solution.py:822
  146.7 15.1 %collective-permute-start.22 = (bf16[8,32,640]{2,1,0:T(8,128)(2,1)S(1)}, bf16[8,32,640]{2,1,0:T(8,128)(2,1)S(1)}, u32[]{:S(2)}, u32[]{:S(2)}) collective-permute-start(bf16[8,32,640]{2,1,0:T(8,128)(2,1)S(1)} %get-tuple-element.155), channel_id=1, source_target_pairs={{0,8},{8,16},{16,24},{1,9},{9,17},{17,25},{2,10},{10,18},{18,26},{... | collective-permute-start | bytes 983048 | tf_op jit(solution)/shard_map/ppermute | solution.py:819
  162.0 28.6 %collective-permute-start.25 = (bf16[2,2,80,1120]{3,2,1,0:T(8,128)(2,1)S(1)}, bf16[2,2,80,1120]{3,2,1,0:T(8,128)(2,1)S(1)}, u32[]{:S(2)}, u32[]{:S(2)}) collective-permute-start(bf16[2,2,80,1120]{3,2,1,0:T(8,128)(2,1)S(1)} %slice_bitcast_fusion), channel_id=1, source_target_pairs={{0,8},{1,9},{2,10},{3,11},{4,12},{5,13},{6,14},{7,15},{8,0},{9,1},... | collective-permute-start | bytes 2150408 | tf_op jit(solution)/shard_map/ppermute | solution.py:50
  167.4 23.4 %collective-permute-start.24 = (bf16[2,2,80,1120]{3,2,1,0:T(8,128)(2,1)S(1)}, bf16[2,2,80,1120]{3,2,1,0:T(8,128)(2,1)S(1)}, u32[]{:S(2)}, u32[]{:S(2)}) collective-permute-start(bf16[2,2,80,1120]{3,2,1,0:T(8,128)(2,1)S(1)} %slice_bitcast_fusion.1), channel_id=1, source_target_pairs={{0,16},{1,17},{2,18},{3,19},{4,20},{5,21},{6,22},{7,23},{8,24},{9,... | collective-permute-start | bytes 2150408 | tf_op jit(solution)/shard_map/ppermute | solution.py:50
  191.1 13.6 %collective-permute-start.27 = (bf16[2,80,1120]{2,1,0:T(8,128)(2,1)S(1)}, bf16[2,80,1120]{2,1,0:T(8,128)(2,1)S(1)}, u32[]{:S(2)}, u32[]{:S(2)}) collective-permute-start(bf16[2,80,1120]{2,1,0:T(8,128)(2,1)S(1)} %slice_bitcast_fusion.2), channel_id=1, source_target_pairs={{0,16},{1,17},{2,18},{3,19},{4,20},{5,21},{6,22},{7,23},{8,24},{9,... | collective-permute-start | bytes 1075208 | tf_op jit(solution)/shard_map/ppermute | solution.py:50
  191.2 13.6 %collective-permute-start.26 = (bf16[2,80,1120]{2,1,0:T(8,128)(2,1)S(1)}, bf16[2,80,1120]{2,1,0:T(8,128)(2,1)S(1)}, u32[]{:S(2)}, u32[]{:S(2)}) collective-permute-start(bf16[2,80,1120]{2,1,0:T(8,128)(2,1)S(1)} %slice_bitcast_fusion.3), channel_id=1, source_target_pairs={{0,8},{1,9},{2,10},{3,11},{4,12},{5,13},{6,14},{7,15},{8,0},{9,1},... | collective-permute-start | bytes 1075208 | tf_op jit(solution)/shard_map/ppermute | solution.py:50
  204.9 21.9 %collective-permute-start.28 = (bf16[80,1120]{1,0:T(8,128)(2,1)S(1)}, bf16[80,1120]{1,0:T(8,128)(2,1)S(1)}, u32[]{:S(2)}, u32[]{:S(2)}) collective-permute-start(bf16[80,1120]{1,0:T(8,128)(2,1)S(1)} %get-tuple-element.160), channel_id=1, source_target_pairs={{0,6},{1,7},{2,0},{3,1},{4,2},{5,3},{6,4},{7,5},{8,14},{9,15},{10,... | collective-permute-start | bytes 537608 | tf_op jit(solution)/shard_map/ppermute | solution.py:50
  206.4 20.4 %collective-permute-start.30 = (bf16[80,1120]{1,0:T(8,128)(2,1)S(1)}, bf16[80,1120]{1,0:T(8,128)(2,1)S(1)}, u32[]{:S(2)}, u32[]{:S(2)}) collective-permute-start(bf16[80,1120]{1,0:T(8,128)(2,1)S(1)} %get-tuple-element.158), channel_id=1, source_target_pairs={{0,2},{1,3},{2,4},{3,5},{4,6},{5,7},{6,0},{7,1},{8,10},{9,11},{10,... | collective-permute-start | bytes 537608 | tf_op jit(solution)/shard_map/ppermute | solution.py:50
  207.5 19.3 %collective-permute-start.29 = (bf16[80,1120]{1,0:T(8,128)(2,1)S(1)}, bf16[80,1120]{1,0:T(8,128)(2,1)S(1)}, u32[]{:S(2)}, u32[]{:S(2)}) collective-permute-start(bf16[80,1120]{1,0:T(8,128)(2,1)S(1)} %get-tuple-element.159), channel_id=1, source_target_pairs={{0,4},{1,5},{2,6},{3,7},{4,0},{5,1},{6,2},{7,3},{8,12},{9,13},{10,... | collective-permute-start | bytes 537608 | tf_op jit(solution)/shard_map/ppermute | solution.py:50
  229.1 9.1 %collective-permute-start.32 = (bf16[2,2,96,320]{3,2,1,0:T(8,128)(2,1)S(1)}, bf16[2,2,96,320]{3,2,1,0:T(8,128)(2,1)S(1)}, u32[]{:S(2)}, u32[]{:S(2)}) collective-permute-start(bf16[2,2,96,320]{3,2,1,0:T(8,128)(2,1)S(1)} %slice_bitcast_fusion.6), channel_id=1, source_target_pairs={{0,16},{1,17},{2,18},{3,19},{4,20},{5,21},{6,22},{7,23},{8,24},{9,... | collective-permute-start | bytes 737288 | tf_op jit(solution)/shard_map/ppermute | solution.py:50
  229.9 9.1 %collective-permute-start.36 = (bf16[2,2,96,320]{3,2,1,0:T(8,128)(2,1)S(1)}, bf16[2,2,96,320]{3,2,1,0:T(8,128)(2,1)S(1)}, u32[]{:S(2)}, u32[]{:S(2)}) collective-permute-start(bf16[2,2,96,320]{3,2,1,0:T(8,128)(2,1)S(1)} %slice_bitcast_fusion.4), channel_id=1, source_target_pairs={{0,8},{1,9},{2,10},{3,11},{4,12},{5,13},{6,14},{7,15},{8,0},{9,1},... | collective-permute-start | bytes 737288 | tf_op jit(solution)/shard_map/ppermute | solution.py:50
  (43 other events, 214.9 us)
